TPU v7x, 32 devices: a whole 2x2x4 slice. The times are simulated.
32 devices in a mesh: gx: 4 (over y, x), gy: 2 (over core), gz: 4 (over z).
Axes of the slice: x: 2, y: 2, z: 4, core: 2. Of those that a mesh axis runs over, the one named last changes fastest.
Arguments:
- ham_blocks: bfloat16 [256, 128, 128], P(('gx', 'gy', 'gz')), may hold values from -0.119628906 to 0.119628906
- onsite: float32 [32, 768], P(('gx', 'gy', 'gz')), may hold values from -1 to 1
- entry_slot: int32 [32, 36], P(('gx', 'gy', 'gz')), may hold values from 0 to 39, as said below
- send_table: int32 [32, 8, 5], P(('gx', 'gy', 'gz')), may hold values from -1 to 7, as said below
- reads: int32 [32, 8], P(('gx', 'gy', 'gz')), may hold values from 0 to 42, as said below
- gram_targets: int32 [32, 7, 8], P(('gx', 'gy', 'gz')), may hold values from 0 to 36, as said below
- table_pick: int32 [32, 2, 8], P(('gx', 'gy', 'gz')), may hold values from 0 to 3, as said below
- phi: bfloat16 [32, 4, 128, 4096], P(('gx', 'gy', 'gz')), may hold values from -2.390625 to 2.390625
- potential_in: float32 [16, 16, 512], P('gx', 'gy', 'gz'), may hold values from -1.5 to 1.5
Outputs:
- potential: float32 [16, 16, 512], P('gx', 'gy', 'gz')
- grid_blocks: float32 [256, 128, 128], P(('gx', 'gy', 'gz'))
Inputs may be any that keep to these rules, and one draw needn't show every extreme that they name: `entry_slot`: row d holds distinct slot numbers; at most 5 entries of one submatrix come from one device of its plane, and some device gives exactly 5. send_table[o, e, c] is the local block that submatrix e of o's plane reads in slot o's plane number * 5 + c, and -1 where e reads no block in that slot. `reads`: 42 marks an unused slot; some brick uses all 8 slots; the number of used slots differs widely between bricks. gram_targets[d, k, r] is 36 where slot r of the brick at face k of d is unused, and an entry below 36 where it is used; one entry of a submatrix receives at most two slots. `table_pick`: the two tables of one slot differ.
All inputs are finite; a program needn't handle non-finite values.
Results may differ from a plain program's by a relative error of at most 0.012.
Values may be sent and summed in bfloat16 or wider, within the bound.
A program may use at most 128 MiB of HBM per device.

v0:
```python
import jax
import jax.numpy as jnp
from jax import lax
from jax.sharding import PartitionSpec as P

B = 128
S = 6
M = 768


EPSILON = 1e-06


def with_halo(cells, sides, width):
    for axis, dim in sides:
        count = lax.axis_size(axis)
        head = lax.slice_in_dim(cells, 0, width, axis=dim)
        tail = lax.slice_in_dim(cells, cells.shape[dim] - width, cells.shape[dim], axis=dim)
        cells = jnp.concatenate(
            [
                lax.ppermute(tail, axis, [(i, (i + 1) % count) for i in range(count)]),
                cells,
                lax.ppermute(head, axis, [((i + 1) % count, i) for i in range(count)]),
            ],
            axis=dim,
        )
    return cells


def density_columns(matrix, onsite_row):
    wide = matrix.astype(jnp.float32)
    hamilton = 0.5 * (wide + wide.T) + jnp.diag(onsite_row)
    factor = lax.rsqrt(jnp.sum(hamilton * hamilton) / M + EPSILON) / 1.3
    start = (hamilton * factor).astype(jnp.bfloat16)
    square = jnp.dot(start, start, preferred_element_type=jnp.float32).astype(jnp.bfloat16)
    cube = jnp.dot(start, square, preferred_element_type=jnp.float32)
    first = (1.5 * start.astype(jnp.float32) - 0.5 * cube).astype(jnp.bfloat16)
    column = first[:, :B]
    inner = jnp.dot(first, column, preferred_element_type=jnp.float32).astype(jnp.bfloat16)
    outer = jnp.dot(first, inner, preferred_element_type=jnp.float32)
    unit = (jnp.arange(M)[:, None] == jnp.arange(B)[None, :]).astype(jnp.float32)
    result = 0.5 * (unit - (1.5 * column.astype(jnp.float32) - 0.5 * outer))
    return result.astype(jnp.bfloat16).reshape(S, B, B)


def face_stack(extended):
    return jnp.stack(
        [
            extended[1, 1, 1],
            extended[0, 1, 1],
            extended[2, 1, 1],
            extended[1, 0, 1],
            extended[1, 2, 1],
            extended[1, 1, 0],
            extended[1, 1, 2],
        ]
    )


def jacobi_step(padded, source):
    beside_all = padded[2:, 1:-1, 1:-1] + padded[:-2, 1:-1, 1:-1]
    beside_all = beside_all + padded[1:-1, 2:, 1:-1] + padded[1:-1, :-2, 1:-1]
    beside_all = beside_all + padded[1:-1, 1:-1, 2:] + padded[1:-1, 1:-1, :-2]
    return (beside_all + source) / 6.0


def shards(
    ham_blocks, onsite, entry_slot, send_table, reads, gram_targets, table_pick, phi, potential_in
):
    plane = lax.axis_size(("gy", "gz"))
    held = ham_blocks.shape[0]
    lanes_count = send_table.shape[2]
    slot_ids = entry_slot[0]
    picks = send_table[0]
    fetched = jnp.take(ham_blocks, jnp.maximum(picks, 0), axis=0)
    outgoing = jnp.where((picks >= 0)[:, :, None, None], fetched, jnp.zeros((), jnp.bfloat16))
    incoming = lax.all_to_all(outgoing, ("gy", "gz"), split_axis=0, concat_axis=0, tiled=True)
    entries = jnp.take(incoming.reshape(plane * lanes_count, B, B), slot_ids, axis=0)
    matrix = entries.reshape(S, S, B, B).transpose(0, 2, 1, 3).reshape(M, M)
    density = density_columns(matrix, onsite[0])
    density_ext = with_halo(density[None, None, None], (("gx", 0), ("gy", 1), ("gz", 2)), 1)
    candidates = jnp.concatenate(
        [face_stack(density_ext).reshape(7 * S, B, B), jnp.zeros((1, B, B), jnp.bfloat16)]
    )
    chosen_blocks = jnp.take(candidates, reads[0], axis=0)
    left_table = jnp.take(phi[0], table_pick[0, 0], axis=0)
    right_table = jnp.take(phi[0], table_pick[0, 1], axis=0)
    mixed = jnp.einsum(
        "rij,rig->rjg", chosen_blocks, left_table, preferred_element_type=jnp.float32
    )
    source = jnp.sum(mixed * right_table, axis=(0, 1)).reshape(potential_in.shape)
    potential = potential_in
    for sweep_index in range(2):
        padded = with_halo(potential, (("gx", 0), ("gy", 1), ("gz", 2)), 1)
        potential = jacobi_step(padded, source)
    weighted = (right_table * potential.reshape(-1)[None, None, :]).astype(jnp.bfloat16)
    grams = jnp.einsum(
        "rig,rjg->rij", left_table, weighted, preferred_element_type=jnp.float32
    ).astype(jnp.bfloat16)
    gram_ext = with_halo(grams[None, None, None], (("gx", 0), ("gy", 1), ("gz", 2)), 1)
    gathered = face_stack(gram_ext).reshape(7 * grams.shape[0], B, B)
    selector = (gram_targets[0].reshape(-1)[None, :] == jnp.arange(S * S)[:, None]).astype(
        jnp.bfloat16
    )
    summed = jnp.einsum(
        "sq,qij->sij", selector, gathered, preferred_element_type=jnp.float32
    ).astype(jnp.bfloat16)
    placement = (jnp.arange(plane * lanes_count)[:, None] == slot_ids[None, :]).astype(jnp.bfloat16)
    outgoing_back = jnp.einsum("qs,sij->qij", placement, summed, preferred_element_type=jnp.float32)
    outgoing_back = outgoing_back.astype(jnp.bfloat16).reshape(plane, lanes_count, B, B)
    arrived = lax.all_to_all(
        outgoing_back, ("gy", "gz"), split_axis=0, concat_axis=0, tiled=True
    ).reshape(plane * lanes_count, B, B)
    owner_select = (send_table[0].reshape(-1)[None, :] == jnp.arange(held)[:, None]).astype(
        jnp.bfloat16
    )
    grid_blocks = jnp.einsum(
        "hq,qij->hij", owner_select, arrived, preferred_element_type=jnp.float32
    )
    return (potential, grid_blocks)


def solution(mesh):
    placed = (
        P(("gx", "gy", "gz"), None, None),
        P(("gx", "gy", "gz"), None),
        P(("gx", "gy", "gz"), None),
        P(("gx", "gy", "gz"), None, None),
        P(("gx", "gy", "gz"), None),
        P(("gx", "gy", "gz"), None, None),
        P(("gx", "gy", "gz"), None, None),
        P(("gx", "gy", "gz"), None, None, None),
        P("gx", "gy", "gz"),
    )
    return jax.shard_map(
        shards,
        mesh=mesh,
        in_specs=placed,
        out_specs=(P("gx", "gy", "gz"), P(("gx", "gy", "gz"), None, None)),
        check_vma=False,
    )
```

profile of v0, /device:TPU:0, one launch (start us, length us, event | category | flops | bytes accessed | tf_op | source)
XLA Modules:
  0.0 359.5 jit_solution(335224166366453054)
XLA Ops:
  3.0 1.3 select_select_fusion
  4.4 6.3 %all-to-all-start = ((bf16[8,5,128,128]{3,2,1,0:T(8,128)(2,1)}), bf16[8,5,128,128]{3,2,1,0:T(8,128)(2,1)S(1)}, u32[]{:S(2)}, u32[]{:S(2)}) async-start(bf16[8,5,128,128]{3,2,1,0:T(8,128)(2,1)} %select_select_fusion), calls=%async_computation | async-start | bytes 2621440 | tf_op jit(solution)/shard_map/all_to_all | solution.py:77
  12.0 30.4 %all-to-all-done = bf16[8,5,128,128]{3,2,1,0:T(8,128)(2,1)S(1)} async-done(((bf16[8,5,128,128]{3,2,1,0:T(8,128)(2,1)}), bf16[8,5,128,128]{3,2,1,0:T(8,128)(2,1)S(1)}, u32[]{:S(2)}, u32[]{:S(2)}) %all-to-all-start) | async-done | bytes 1310752 | tf_op jit(solution)/shard_map/all_to_all | solution.py:77
  43.4 1.4 copy.19
  44.8 2.0 copy.40
  46.8 3.1 copy.20
  49.9 3.1 multiply_reduce_fusion
  53.6 9.0 %subtract_convert_fusion = bf16[768,768]{1,0:T(8,128)(2,1)S(1)} fusion(f32[]{:T(128)S(6)} %div.13, f32[768]{0:T(1024)S(1)} %reduce.1, f32[768,768]{1,0:T(8,128)} %bitcast.124, f32[768,768]{0,1:T(8,128)} %copy.20), kind=kOutput, calls=%fused_computation.19 | convolution fusion | flops 1827864576 | bytes 5901316 | tf_op jit(solution)/shard_map/dot_general | solution.py:36
  62.6 1.3 fusion.22
  64.0 2.5 collective-permute-start.7
  66.5 2.9 collective-permute-start
  69.4 2.3 collective-permute-done.7
  71.8 4.6 %collective-permute-done.6 = bf16[1,1,1,6,128,128]{5,4,3,2,1,0:T(8,128)(2,1)S(1)} collective-permute-done((bf16[1,1,1,6,128,128]{5,4,3,2,1,0:T(8,128)(2,1)S(1)}, bf16[1,1,1,6,128,128]{5,4,3,2,1,0:T(8,128)(2,1)S(1)}, u32[]{:S(2)}, u32[]{:S(2)}) %collective-permute-start.6) | collective-permute-done | bytes 196640 | tf_op jit(solution)/shard_map/ppermute | solution.py:21
  77.1 1.4 collective-permute-done.9
  79.7 3.8 %collective-permute-start.11 = (bf16[3,3,1,6,128,128]{5,4,3,2,1,0:T(8,128)(2,1)S(1)}, bf16[3,3,1,6,128,128]{5,4,3,2,1,0:T(8,128)(2,1)}, u32[]{:S(2)}, u32[]{:S(2)}) collective-permute-start(bf16[3,3,1,6,128,128]{5,4,3,2,1,0:T(8,128)(2,1)S(1)} %pad_maximum_fusion.1), channel_id=1, source_target_pairs={{1,0},{2,1},{3,2},{0,3},{5,4},{6,5},{7,6},{4,7},{9,8},{10,9},{11,1... | collective-permute-start | bytes 5308424 | tf_op jit(solution)/shard_map/ppermute | solution.py:23
  84.1 6.9 %gather_fusion.4 = bf16[8,128,4096]{2,1,0:T(8,128)(2,1)} fusion(bf16[4,128,4096]{2,1,0:T(8,128)(2,1)} %bitcast.119, s32[1024]{0:T(1024)S(1)} %get-tuple-element.29), kind=kCustom, calls=%fused_computation.1.clone | custom fusion | bytes 16777248 | tf_op jit(solution)/shard_map/jit(_take)/gather | solution.py:87
  91.0 6.8 %gather_fusion.3 = bf16[8,128,4096]{2,1,0:T(8,128)(2,1)} fusion(bf16[4,128,4096]{2,1,0:T(8,128)(2,1)} %bitcast.120, s32[1024]{0:T(1024)S(1)} %get-tuple-element.30), kind=kCustom, calls=%fused_computation.clone | custom fusion | bytes 16777248 | tf_op jit(solution)/shard_map/jit(_take)/gather | solution.py:86
  97.9 2.0 collective-permute-start.5
  100.0 1.0 fusion.32
  101.0 22.0 %collective-permute-done.10 = bf16[3,3,1,6,128,128]{5,4,3,2,1,0:T(8,128)(2,1)} collective-permute-done((bf16[3,3,1,6,128,128]{5,4,3,2,1,0:T(8,128)(2,1)S(1)}, bf16[3,3,1,6,128,128]{5,4,3,2,1,0:T(8,128)(2,1)}, u32[]{:S(2)}, u32[]{:S(2)}) %collective-permute-start.10) | collective-permute-done | bytes 1769504 | tf_op jit(solution)/shard_map/ppermute | solution.py:21
  123.0 1.0 fusion.30
  124.0 34.9 %collective-permute-done.11 = bf16[3,3,1,6,128,128]{5,4,3,2,1,0:T(8,128)(2,1)} collective-permute-done((bf16[3,3,1,6,128,128]{5,4,3,2,1,0:T(8,128)(2,1)S(1)}, bf16[3,3,1,6,128,128]{5,4,3,2,1,0:T(8,128)(2,1)}, u32[]{:S(2)}, u32[]{:S(2)}) %collective-permute-start.11) | collective-permute-done | bytes 1769504 | tf_op jit(solution)/shard_map/ppermute | solution.py:23
  158.9 1.0 fusion.29
  160.7 9.4 %fusion = f32[4096]{0:T(1024)S(1)} fusion(bf16[8,128,4096]{2,1,0:T(8,128)(2,1)} %gather_fusion.3, pred[8]{0:T(512)(128)(4,1)S(1)} %get-tuple-element.25, bf16[8,128,4096]{2,1,0:T(8,128)(2,1)} %gather_fusion.4, pred[8]{0:T(512)(128)(4,1)S(1)} %get-tuple-element.7, bf16[8,128,128]{2,1,0:T(8,128)(2,1)S(1)} %gather_fusion.2, pred[8]{0:T(512)(128)(4,1)S(1)} %compare_and_fusion.3), kind=kOutput, calls=%fused_computation.7 | convolution fusion | flops 1094840320 | bytes 17055768 | tf_op jit(solution)/shard_map/rij,rig->rjg/dot_general | solution.py:88
  170.2 1.5 collective-permute-start.13
  171.7 1.4 collective-permute-start.12
  173.2 1.6 collective-permute-done.13
  176.8 2.1 collective-permute-start.16
  178.8 2.0 collective-permute-done.16
  180.9 3.8 %collective-permute-done.17 = f32[6,10,1]{2,1,0:T(8,128)S(1)} collective-permute-done((f32[6,10,1]{2,1,0:T(8,128)S(1)}, f32[6,10,1]{2,1,0:T(8,128)S(1)}, u32[]{:S(2)}, u32[]{:S(2)}) %collective-permute-start.17) | collective-permute-done | bytes 272 | tf_op jit(solution)/shard_map/ppermute | solution.py:21
  184.8 9.1 %bitcast_dynamic-update-slice_fusion.2 = (bf16[7,8,128,128]{3,2,1,0:T(8,128)(2,1)}, bf16[8,128,128]{2,1,0:T(8,128)(2,1)S(1)}) fusion(f32[4096]{0:T(1024)S(1)} %fusion.74, bf16[8,128,4096]{2,1,0:T(8,128)(2,1)} %gather_fusion.4, pred[8]{0:T(512)(128)(4,1)S(1)} %get-tuple-element.7, bf16[8,128,4096]{2,1,0:T(8,128)(2,1)} %gather_fusion.3, ...), kind=kOutput, calls=%fused_computation.52 | convolution fusion | flops 1094844416 | bytes 17317904 | tf_op jit(solution)/shard_map/rig,rjg->rij/dot_general | solution.py:97
  194.0 2.3 collective-permute-start.19
  196.3 6.9 %collective-permute-done.19 = bf16[1,1,1,8,128,128]{5,4,3,2,1,0:T(8,128)(2,1)S(1)} collective-permute-done((bf16[1,1,1,8,128,128]{5,4,3,2,1,0:T(8,128)(2,1)S(1)}, bf16[1,1,1,8,128,128]{5,4,3,2,1,0:T(8,128)(2,1)S(1)}, u32[]{:S(2)}, u32[]{:S(2)}) %collective-permute-start.19) | collective-permute-done | bytes 262176 | tf_op jit(solution)/shard_map/ppermute | solution.py:23
  203.2 4.1 %collective-permute-done.18 = bf16[1,1,1,8,128,128]{5,4,3,2,1,0:T(8,128)(2,1)S(1)} collective-permute-done((bf16[1,1,1,8,128,128]{5,4,3,2,1,0:T(8,128)(2,1)S(1)}, bf16[1,1,1,8,128,128]{5,4,3,2,1,0:T(8,128)(2,1)S(1)}, u32[]{:S(2)}, u32[]{:S(2)}) %collective-permute-start.18) | collective-permute-done | bytes 262176 | tf_op jit(solution)/shard_map/ppermute | solution.py:21
  208.0 1.8 collective-permute-done.21
  209.8 1.1 collective-permute-done.20
  211.8 3.8 %collective-permute-start.23 = (bf16[3,3,1,8,128,128]{5,4,3,2,1,0:T(8,128)(2,1)S(1)}, bf16[3,3,1,8,128,128]{5,4,3,2,1,0:T(8,128)(2,1)}, u32[]{:S(2)}, u32[]{:S(2)}) collective-permute-start(bf16[3,3,1,8,128,128]{5,4,3,2,1,0:T(8,128)(2,1)S(1)} %pad_maximum_fusion), channel_id=1, source_target_pairs={{1,0},{2,1},{3,2},{0,3},{5,4},{6,5},{7,6},{4,7},{9,8},{10,9},{11,1... | collective-permute-start | bytes 7077896 | tf_op jit(solution)/shard_map/ppermute | solution.py:23
  217.1 1.7 fusion.26
  218.8 1.7 fusion.25
  220.5 47.3 %collective-permute-done.22 = bf16[3,3,1,8,128,128]{5,4,3,2,1,0:T(8,128)(2,1)} collective-permute-done((bf16[3,3,1,8,128,128]{5,4,3,2,1,0:T(8,128)(2,1)S(1)}, bf16[3,3,1,8,128,128]{5,4,3,2,1,0:T(8,128)(2,1)}, u32[]{:S(2)}, u32[]{:S(2)}) %collective-permute-start.22) | collective-permute-done | bytes 2359328 | tf_op jit(solution)/shard_map/ppermute | solution.py:21
  267.8 1.7 fusion.24
  269.5 46.3 %collective-permute-done.23 = bf16[3,3,1,8,128,128]{5,4,3,2,1,0:T(8,128)(2,1)} collective-permute-done((bf16[3,3,1,8,128,128]{5,4,3,2,1,0:T(8,128)(2,1)S(1)}, bf16[3,3,1,8,128,128]{5,4,3,2,1,0:T(8,128)(2,1)}, u32[]{:S(2)}, u32[]{:S(2)}) %collective-permute-start.23) | collective-permute-done | bytes 2359328 | tf_op jit(solution)/shard_map/ppermute | solution.py:23
  315.7 1.7 fusion.23
  317.4 3.4 convolution_convert_fusion
  320.9 1.4 copy.23
  322.3 3.7 %all-to-all-start.1 = ((bf16[8,5,128,128]{3,2,1,0:T(8,128)(2,1)}), bf16[8,5,128,128]{3,2,1,0:T(8,128)(2,1)S(1)}, u32[]{:S(2)}, u32[]{:S(2)}) async-start(bf16[8,5,128,128]{3,2,1,0:T(8,128)(2,1)} %bitcast.39), calls=%async_computation.1 | async-start | bytes 2621440 | tf_op jit(solution)/shard_map/all_to_all | solution.py:111
  326.7 31.0 %all-to-all-done.1 = bf16[8,5,128,128]{3,2,1,0:T(8,128)(2,1)S(1)} async-done(((bf16[8,5,128,128]{3,2,1,0:T(8,128)(2,1)}), bf16[8,5,128,128]{3,2,1,0:T(8,128)(2,1)S(1)}, u32[]{:S(2)}, u32[]{:S(2)}) %all-to-all-start.1) | async-done | bytes 1310752 | tf_op jit(solution)/shard_map/all_to_all | solution.py:111
  357.7 0.9 fusion.14
  (94 shorter events, 15.0 us)
Async XLA Ops:
  0.6 1.6 copy-start
  3.0 8.2 %copy-start.8 = (s32[1,36]{1,0:T(1,128)S(1)}, s32[1,36]{1,0:T(1,128)}, u32[]{:S(2)}) copy-start(s32[1,36]{1,0:T(1,128)} %param.13) | copy-start | bytes 436
  3.0 8.9 %copy-start.6 = (f32[1,768]{1,0:T(1,128)S(1)}, f32[1,768]{1,0:T(1,128)}, u32[]{:S(2)}) copy-start(f32[1,768]{1,0:T(1,128)} %param.12) | copy-start | bytes 9220
  4.4 38.1 %all-to-all-start = ((bf16[8,5,128,128]{3,2,1,0:T(8,128)(2,1)}), bf16[8,5,128,128]{3,2,1,0:T(8,128)(2,1)S(1)}, u32[]{:S(2)}, u32[]{:S(2)}) async-start(bf16[8,5,128,128]{3,2,1,0:T(8,128)(2,1)} %select_select_fusion), calls=%async_computation | async-start | bytes 2621440 | tf_op jit(solution)/shard_map/all_to_all | solution.py:77
  62.6 3.9 %copy-start.4 = (f32[4,8,128]{2,1,0:T(8,128)S(1)}, f32[4,8,128]{2,1,0:T(8,128)}, u32[]{:S(2)}) copy-start(f32[4,8,128]{2,1,0:T(8,128)} %param.19) | copy-start | bytes 49156
  62.6 14.4 %copy-start.7 = (s32[1,2,8]{2,1,0:T(2,128)S(1)}, s32[1,2,8]{2,1,0:T(2,128)}, u32[]{:S(2)}) copy-start(s32[1,2,8]{2,1,0:T(2,128)} %param.17) | copy-start | bytes 196
  62.6 14.4 %copy-start.9 = (s32[1,8]{1,0:T(1,128)S(1)}, s32[1,8]{1,0:T(1,128)}, u32[]{:S(2)}) copy-start(s32[1,8]{1,0:T(1,128)} %param.15) | copy-start | bytes 100
  64.0 7.8 %collective-permute-start.7 = (bf16[1,1,1,6,128,128]{5,4,3,2,1,0:T(8,128)(2,1)S(1)}, bf16[1,1,1,6,128,128]{5,4,3,2,1,0:T(8,128)(2,1)S(1)}, u32[]{:S(2)}, u32[]{:S(2)}) collective-permute-start(bf16[1,1,1,6,128,128]{5,4,3,2,1,0:T(8,128)(2,1)S(1)} %bitcast.131), channel_id=1, source_target_pairs={{8,0},{16,8},{24,16},{0,24},{9,1},{17,9},{25,17},{1,25},{10,2},{18... | collective-permute-start | bytes 589832 | tf_op jit(solution)/shard_map/ppermute | solution.py:23
  66.5 9.9 %collective-permute-start.6 = (bf16[1,1,1,6,128,128]{5,4,3,2,1,0:T(8,128)(2,1)S(1)}, bf16[1,1,1,6,128,128]{5,4,3,2,1,0:T(8,128)(2,1)S(1)}, u32[]{:S(2)}, u32[]{:S(2)}) collective-permute-start(bf16[1,1,1,6,128,128]{5,4,3,2,1,0:T(8,128)(2,1)S(1)} %bitcast.132), channel_id=1, source_target_pairs={{0,8},{8,16},{16,24},{24,0},{1,9},{9,17},{17,25},{25,1},{2,10},{10... | collective-permute-start | bytes 589832 | tf_op jit(solution)/shard_map/ppermute | solution.py:21
  66.5 13.2 %collective-permute-start = (f32[1,8,128]{2,1,0:T(8,128)S(1)}, f32[1,8,128]{2,1,0:T(8,128)S(1)}, u32[]{:S(2)}, u32[]{:S(2)}) collective-permute-start(f32[1,8,128]{2,1,0:T(8,128)S(1)} %get-tuple-element.21), channel_id=1, source_target_pairs={{8,0},{16,8},{24,16},{0,24},{9,1},{17,9},{25,17},{1,25},{10,2},{18... | collective-permute-start | bytes 12296 | tf_op jit(solution)/shard_map/ppermute | solution.py:23
  69.4 7.7 %collective-permute-start.1 = (f32[1,8,128]{2,1,0:T(8,128)S(1)}, f32[1,8,128]{2,1,0:T(8,128)S(1)}, u32[]{:S(2)}, u32[]{:S(2)}) collective-permute-start(f32[1,8,128]{2,1,0:T(8,128)S(1)} %get-tuple-element.22), channel_id=1, source_target_pairs={{0,8},{8,16},{16,24},{24,0},{1,9},{9,17},{17,25},{25,1},{2,10},{10... | collective-permute-start | bytes 12296 | tf_op jit(solution)/shard_map/ppermute | solution.py:21
  76.5 2.1 collective-permute-start.9
  76.5 2.8 collective-permute-start.8
  79.4 4.1 %copy-start.3 = (bf16[3,1,1,6,128,128]{5,4,3,2,1,0:T(8,128)(2,1)}, bf16[3,1,1,6,128,128]{5,4,3,2,1,0:T(8,128)(2,1)S(1)}, u32[]{:S(2)}) copy-start(bf16[3,1,1,6,128,128]{5,4,3,2,1,0:T(8,128)(2,1)S(1)} %collective-permute-done.8) | copy-start | bytes 1769476
  79.6 43.5 %collective-permute-start.10 = (bf16[3,3,1,6,128,128]{5,4,3,2,1,0:T(8,128)(2,1)S(1)}, bf16[3,3,1,6,128,128]{5,4,3,2,1,0:T(8,128)(2,1)}, u32[]{:S(2)}, u32[]{:S(2)}) collective-permute-start(bf16[3,3,1,6,128,128]{5,4,3,2,1,0:T(8,128)(2,1)S(1)} %pad_maximum_fusion.1), channel_id=1, source_target_pairs={{0,1},{1,2},{2,3},{3,0},{4,5},{5,6},{6,7},{7,4},{8,9},{9,10},{10,1... | collective-permute-start | bytes 5308424 | tf_op jit(solution)/shard_map/ppermute | solution.py:21
  79.7 79.3 %collective-permute-start.11 = (bf16[3,3,1,6,128,128]{5,4,3,2,1,0:T(8,128)(2,1)S(1)}, bf16[3,3,1,6,128,128]{5,4,3,2,1,0:T(8,128)(2,1)}, u32[]{:S(2)}, u32[]{:S(2)}) collective-permute-start(bf16[3,3,1,6,128,128]{5,4,3,2,1,0:T(8,128)(2,1)S(1)} %pad_maximum_fusion.1), channel_id=1, source_target_pairs={{1,0},{2,1},{3,2},{0,3},{5,4},{6,5},{7,6},{4,7},{9,8},{10,9},{11,1... | collective-permute-start | bytes 5308424 | tf_op jit(solution)/shard_map/ppermute | solution.py:23
  83.5 14.3 %collective-permute-start.3 = (f32[6,1,128]{2,1,0:T(1,128)S(1)}, f32[6,1,128]{2,1,0:T(1,128)S(1)}, u32[]{:S(2)}, u32[]{:S(2)}) collective-permute-start(f32[6,1,128]{2,1,0:T(1,128)S(1)} %get-tuple-element.17), channel_id=1, source_target_pairs={{0,4},{4,0},{1,5},{5,1},{2,6},{6,2},{3,7},{7,3},{8,12},{12,8},{9,1... | collective-permute-start | bytes 9224 | tf_op jit(solution)/shard_map/ppermute | solution.py:21
  83.6 14.2 %collective-permute-start.2 = (f32[6,1,128]{2,1,0:T(1,128)S(1)}, f32[6,1,128]{2,1,0:T(1,128)S(1)}, u32[]{:S(2)}, u32[]{:S(2)}) collective-permute-start(f32[6,1,128]{2,1,0:T(1,128)S(1)} %get-tuple-element.18), channel_id=1, source_target_pairs={{4,0},{0,4},{5,1},{1,5},{6,2},{2,6},{7,3},{3,7},{12,8},{8,12},{13,... | collective-permute-start | bytes 9224 | tf_op jit(solution)/shard_map/ppermute | solution.py:23
  97.9 72.2 %collective-permute-start.4 = (f32[6,10,1]{2,1,0:T(8,128)S(1)}, f32[6,10,1]{2,1,0:T(8,128)S(1)}, u32[]{:S(2)}, u32[]{:S(2)}) collective-permute-start(f32[6,10,1]{2,1,0:T(8,128)S(1)} %get-tuple-element.13), channel_id=1, source_target_pairs={{1,0},{2,1},{3,2},{0,3},{5,4},{6,5},{7,6},{4,7},{9,8},{10,9},{11,1... | collective-permute-start | bytes 728 | tf_op jit(solution)/shard_map/ppermute | solution.py:23
  97.9 72.2 %collective-permute-start.5 = (f32[6,10,1]{2,1,0:T(8,128)S(1)}, f32[6,10,1]{2,1,0:T(8,128)S(1)}, u32[]{:S(2)}, u32[]{:S(2)}) collective-permute-start(f32[6,10,1]{2,1,0:T(8,128)S(1)} %get-tuple-element.14), channel_id=1, source_target_pairs={{0,1},{1,2},{2,3},{3,0},{4,5},{5,6},{6,7},{7,4},{8,9},{9,10},{10,1... | collective-permute-start | bytes 728 | tf_op jit(solution)/shard_map/ppermute | solution.py:21
  170.2 4.6 %collective-permute-start.13 = (f32[1,8,128]{2,1,0:T(8,128)S(1)}, f32[1,8,128]{2,1,0:T(8,128)S(1)}, u32[]{:S(2)}, u32[]{:S(2)}) collective-permute-start(f32[1,8,128]{2,1,0:T(8,128)S(1)} %get-tuple-element.19), channel_id=1, source_target_pairs={{0,8},{8,16},{16,24},{24,0},{1,9},{9,17},{17,25},{25,1},{2,10},{10... | collective-permute-start | bytes 12296 | tf_op jit(solution)/shard_map/ppermute | solution.py:21
  171.7 3.6 %collective-permute-start.12 = (f32[1,8,128]{2,1,0:T(8,128)S(1)}, f32[1,8,128]{2,1,0:T(8,128)S(1)}, u32[]{:S(2)}, u32[]{:S(2)}) collective-permute-start(f32[1,8,128]{2,1,0:T(8,128)S(1)} %get-tuple-element.20), channel_id=1, source_target_pairs={{8,0},{16,8},{24,16},{0,24},{9,1},{17,9},{25,17},{1,25},{10,2},{18... | collective-permute-start | bytes 12296 | tf_op jit(solution)/shard_map/ppermute | solution.py:23
  175.4 1.2 collective-permute-start.15
  175.4 1.3 collective-permute-start.14
  176.8 4.1 %collective-permute-start.16 = (f32[6,10,1]{2,1,0:T(8,128)S(1)}, f32[6,10,1]{2,1,0:T(8,128)S(1)}, u32[]{:S(2)}, u32[]{:S(2)}) collective-permute-start(f32[6,10,1]{2,1,0:T(8,128)S(1)} %get-tuple-element.11), channel_id=1, source_target_pairs={{1,0},{2,1},{3,2},{0,3},{5,4},{6,5},{7,6},{4,7},{9,8},{10,9},{11,1... | collective-permute-start | bytes 728 | tf_op jit(solution)/shard_map/ppermute | solution.py:23
  178.8 5.9 %collective-permute-start.17 = (f32[6,10,1]{2,1,0:T(8,128)S(1)}, f32[6,10,1]{2,1,0:T(8,128)S(1)}, u32[]{:S(2)}, u32[]{:S(2)}) collective-permute-start(f32[6,10,1]{2,1,0:T(8,128)S(1)} %get-tuple-element.12), channel_id=1, source_target_pairs={{0,1},{1,2},{2,3},{3,0},{4,5},{5,6},{6,7},{7,4},{8,9},{9,10},{10,1... | collective-permute-start | bytes 728 | tf_op jit(solution)/shard_map/ppermute | solution.py:21
  194.0 9.2 %collective-permute-start.19 = (bf16[1,1,1,8,128,128]{5,4,3,2,1,0:T(8,128)(2,1)S(1)}, bf16[1,1,1,8,128,128]{5,4,3,2,1,0:T(8,128)(2,1)S(1)}, u32[]{:S(2)}, u32[]{:S(2)}) collective-permute-start(bf16[1,1,1,8,128,128]{5,4,3,2,1,0:T(8,128)(2,1)S(1)} %bitcast.136), channel_id=1, source_target_pairs={{8,0},{16,8},{24,16},{0,24},{9,1},{17,9},{25,17},{1,25},{10,2},{18... | collective-permute-start | bytes 786440 | tf_op jit(solution)/shard_map/ppermute | solution.py:23
  196.3 11.0 %collective-permute-start.18 = (bf16[1,1,1,8,128,128]{5,4,3,2,1,0:T(8,128)(2,1)S(1)}, bf16[1,1,1,8,128,128]{5,4,3,2,1,0:T(8,128)(2,1)S(1)}, u32[]{:S(2)}, u32[]{:S(2)}) collective-permute-start(bf16[1,1,1,8,128,128]{5,4,3,2,1,0:T(8,128)(2,1)S(1)} %bitcast.137), channel_id=1, source_target_pairs={{0,8},{8,16},{16,24},{24,0},{1,9},{9,17},{17,25},{25,1},{2,10},{10... | collective-permute-start | bytes 786440 | tf_op jit(solution)/shard_map/ppermute | solution.py:21
  207.4 8.2 %copy-start.5 = (s32[1,7,8]{2,0,1:T(1,128)S(1)}, s32[1,7,8]{2,0,1:T(1,128)}, u32[]{:S(2)}) copy-start(s32[1,7,8]{2,0,1:T(1,128)} %param.16) | copy-start | bytes 676
  207.4 2.4 collective-permute-start.21
  207.5 3.4 collective-permute-start.20
  209.8 1.4 copy-start.1
  210.9 0.9 copy-start.2
  211.8 56.0 %collective-permute-start.22 = (bf16[3,3,1,8,128,128]{5,4,3,2,1,0:T(8,128)(2,1)S(1)}, bf16[3,3,1,8,128,128]{5,4,3,2,1,0:T(8,128)(2,1)}, u32[]{:S(2)}, u32[]{:S(2)}) collective-permute-start(bf16[3,3,1,8,128,128]{5,4,3,2,1,0:T(8,128)(2,1)S(1)} %pad_maximum_fusion), channel_id=1, source_target_pairs={{0,1},{1,2},{2,3},{3,0},{4,5},{5,6},{6,7},{7,4},{8,9},{9,10},{10,1... | collective-permute-start | bytes 7077896 | tf_op jit(solution)/shard_map/ppermute | solution.py:21
  211.8 104.0 %collective-permute-start.23 = (bf16[3,3,1,8,128,128]{5,4,3,2,1,0:T(8,128)(2,1)S(1)}, bf16[3,3,1,8,128,128]{5,4,3,2,1,0:T(8,128)(2,1)}, u32[]{:S(2)}, u32[]{:S(2)}) collective-permute-start(bf16[3,3,1,8,128,128]{5,4,3,2,1,0:T(8,128)(2,1)S(1)} %pad_maximum_fusion), channel_id=1, source_target_pairs={{1,0},{2,1},{3,2},{0,3},{5,4},{6,5},{7,6},{4,7},{9,8},{10,9},{11,1... | collective-permute-start | bytes 7077896 | tf_op jit(solution)/shard_map/ppermute | solution.py:23
  322.3 35.4 %all-to-all-start.1 = ((bf16[8,5,128,128]{3,2,1,0:T(8,128)(2,1)}), bf16[8,5,128,128]{3,2,1,0:T(8,128)(2,1)S(1)}, u32[]{:S(2)}, u32[]{:S(2)}) async-start(bf16[8,5,128,128]{3,2,1,0:T(8,128)(2,1)} %bitcast.39), calls=%async_computation.1 | async-start | bytes 2621440 | tf_op jit(solution)/shard_map/all_to_all | solution.py:111
where the time goes:
time: 360 us; the launch traced here: 359 us
  waiting for transfers between devices  244 us (68%)
  local copies, waits for them, and re-layouts  38.3 us (11%)
  starting transfers between devices  34.7 us (10%)
  matrix products  33.2 us (9%)
  other arithmetic  7.58 us (2%)
    ppermute x12, waiting for transfers between devices, with_halo(): lax.ppermute(head, axis, [((i + 1) % count, i) for i in range(count)])  96.5 us
    ppermute x12, waiting for transfers between devices, with_halo(): lax.ppermute(tail, axis, [(i, (i + 1) % count) for i in range(count)])  86.1 us
    all_to_all x1, waiting for transfers between devices, shards(): lax.all_to_all(outgoing_back, ('gy', 'gz'), split_axis=0, concat_axis=0,...  31 us
    all_to_all x1, waiting for transfers between devices, shards(): lax.all_to_all(outgoing, ('gy', 'gz'), split_axis=0, concat_axis=0, tiled...  30.4 us
    ppermute x12, starting transfers between devices, with_halo(): lax.ppermute(head, axis, [((i + 1) % count, i) for i in range(count)])  20 us
    unnamed x37, local copies, waits for them, and re-layouts  13.3 us
    dot_general x1, matrix products, shards(): jnp.einsum('rij,rig->rjg', chosen_blocks, left_table, preferred_element_t...  9.37 us
    dot_general x1, matrix products, shards(): jnp.einsum('rig,rjg->rij', left_table, weighted, preferred_element_type=j...  9.15 us
  transfers between devices with their start and end apart: 26, of which 20 were waited for; matrix products, arithmetic and copies ran while one was open for 10% of the time, Pallas kernels for 0%

commit v1 on v0

v1 whole, which is shorter than its diff:
```python
import functools

import jax
import jax.numpy as jnp
from jax import lax
from jax.experimental import pallas as pl
from jax.experimental.pallas import tpu as pltpu
from jax.sharding import PartitionSpec as P

EPSILON = 1e-06
PLANE = ("gy", "gz")
EVERY = ("gx", "gy", "gz")
VMEM_LIMIT = 48 * 1024 * 1024
VMEM = pl.BlockSpec(memory_space=pltpu.VMEM)
SMEM = pl.BlockSpec(memory_space=pltpu.SMEM)


def local_call(kernel, out_shape, in_specs, scratch=(), flops=0, moved=0):
    return pl.pallas_call(
        kernel,
        out_shape=out_shape,
        in_specs=in_specs,
        out_specs=VMEM,
        scratch_shapes=scratch,
        compiler_params=pltpu.CompilerParams(vmem_limit_bytes=VMEM_LIMIT),
        cost_estimate=pl.CostEstimate(flops=flops, bytes_accessed=moved, transcendentals=0),
    )


def density_kernel(side, bins_ref, blocks_ref, onsite_ref, out_ref, h_ref, x_ref, q_ref):
    width = blocks_ref.shape[1]
    order = side * width
    rows = lax.broadcasted_iota(jnp.int32, (width, width), 0)
    columns = lax.broadcasted_iota(jnp.int32, (width, width), 1)
    unit = rows == columns
    total = jnp.zeros((width, width), jnp.float32)
    for s in range(side):
        for t in range(s, side):
            upper = blocks_ref[bins_ref[s * side + t]].astype(jnp.float32)
            lower = blocks_ref[bins_ref[t * side + s]].astype(jnp.float32)
            block = 0.5 * (upper + lower.T)
            here, there = pl.ds(s * width, width), pl.ds(t * width, width)
            if s == t:
                block = block + jnp.where(unit, onsite_ref[:, here], 0.0)
                total = total + block * block
            else:
                total = total + 2.0 * (block * block)
                h_ref[there, here] = block.T
            h_ref[here, there] = block
    norm = jnp.sum(jnp.sum(total, axis=0, keepdims=True), axis=1, keepdims=True)
    factor = lax.rsqrt(norm / order + EPSILON) / 1.3
    for s in range(side):
        here = pl.ds(s * width, width)
        x_ref[here, :] = (h_ref[here, :] * factor).astype(jnp.bfloat16)
    step = 256 if order % 256 == 0 else width
    for c in range(order // step):
        here = pl.ds(c * step, step)
        q_ref[:, here] = jnp.dot(
            x_ref[...], x_ref[:, here], preferred_element_type=jnp.float32
        ).astype(jnp.bfloat16)
    for c in range(order // step):
        here = pl.ds(c * step, step)
        h_ref[:, here] = 1.5 * x_ref[:, here].astype(jnp.float32) - 0.5 * jnp.dot(
            x_ref[...], q_ref[:, here], preferred_element_type=jnp.float32
        )
    for c in range(order // step):
        here = pl.ds(c * step, step)
        q_ref[:, here] = h_ref[:, here].astype(jnp.bfloat16)
    first = q_ref[...]
    column = q_ref[:, :width]
    inner = jnp.dot(first, column, preferred_element_type=jnp.float32).astype(jnp.bfloat16)
    outer = jnp.dot(first, inner, preferred_element_type=jnp.float32)
    result = -0.5 * (1.5 * column.astype(jnp.float32) - 0.5 * outer)
    for s in range(side):
        part = result[s * width : (s + 1) * width, :]
        if s == 0:
            part = part + jnp.where(unit, 0.5, 0.0)
        out_ref[s] = part.astype(jnp.bfloat16)


def source_kernel(reads_ref, pick_ref, blocks_ref, phi_ref, out_ref, p_ref, pb_ref):
    width = blocks_ref.shape[1]
    count = blocks_ref.shape[0]
    tables = phi_ref.shape[0]
    points = phi_ref.shape[2]
    p_ref[...] = jnp.zeros_like(p_ref)
    for r in range(reads_ref.shape[0]):
        code = reads_ref[r]

        @pl.when(code < count)
        def _():
            place = pick_ref[0, r] * tables + pick_ref[1, r]
            p_ref[place] = p_ref[place] + blocks_ref[code].astype(jnp.float32)

    for a in range(tables):
        for b in range(tables):
            pb_ref[a * width : (a + 1) * width, b * width : (b + 1) * width] = p_ref[
                a * tables + b
            ].astype(jnp.bfloat16)
    step = 512

    def body(c, carry):
        here = pl.ds(pl.multiple_of(c * step, step), step)
        cells = phi_ref[:, :, here].reshape(tables * width, step)
        mixed = jnp.dot(pb_ref[...], cells, preferred_element_type=jnp.float32)
        line = jnp.sum(mixed * cells.astype(jnp.float32), axis=0, keepdims=True)
        for j in range(step // 128):
            out_ref[pl.ds(c * (step // 128) + j, 1), :] = line[:, j * 128 : (j + 1) * 128]
        return carry

    lax.fori_loop(0, points // step, body, 0)


def pairs_of(tables):
    return [(a, b) for a in range(tables) for b in range(a + 1, tables)]


def gram_kernel(phi_ref, v_ref, out_ref, g_ref):
    tables, width, points = phi_ref.shape
    step = 512
    g_ref[...] = jnp.zeros_like(g_ref)
    size = (tables - 1) * width

    def body(c, carry):
        here = pl.ds(pl.multiple_of(c * step, step), step)
        rows = v_ref[pl.ds(c * (step // 128), step // 128), :]
        line = jnp.concatenate([rows[j : j + 1, :] for j in range(step // 128)], axis=1)
        right = phi_ref[1:, :, here].reshape(size, step).astype(jnp.float32)
        weighted = (right * line).astype(jnp.bfloat16)
        left = phi_ref[: tables - 1, :, here].reshape(size, step)
        g_ref[...] += lax.dot_general(
            left, weighted, (((1,), (1,)), ((), ())), preferred_element_type=jnp.float32
        )
        return carry

    lax.fori_loop(0, points // step, body, 0)
    for n, (a, b) in enumerate(pairs_of(tables)):
        out_ref[n] = g_ref[
            a * width : (a + 1) * width, (b - 1) * width : b * width
        ].astype(jnp.bfloat16)


def combine_kernel(bin_ref, col_ref, flip_ref, blocks_ref, out_ref, acc_ref):
    bins = out_ref.shape[0]
    acc_ref[...] = jnp.zeros_like(acc_ref)

    def body(n, carry):
        place = bin_ref[n]

        @pl.when((place < bins) & (flip_ref[n] == 0))
        def _():
            acc_ref[place] = acc_ref[place] + blocks_ref[col_ref[n]].astype(jnp.float32)

        @pl.when((place < bins) & (flip_ref[n] == 1))
        def _():
            acc_ref[place] = acc_ref[place] + blocks_ref[col_ref[n]].astype(jnp.float32).T

        return carry

    lax.fori_loop(0, bin_ref.shape[0], body, 0)
    out_ref[...] = acc_ref[...].astype(jnp.bfloat16)


def both_sides(low_part, high_part, axis):
    count = lax.axis_size(axis)
    if count == 1:
        return high_part, low_part
    up = [(i, (i + 1) % count) for i in range(count)]
    down = [((i + 1) % count, i) for i in range(count)]
    below = lax.ppermute(high_part, axis, up)
    if count == 2 and low_part is high_part:
        return below, below
    return below, lax.ppermute(low_part, axis, down)


def face_stack(block):
    parts = [block]
    for axis in EVERY:
        parts.extend(both_sides(block, block, axis))
    return jnp.concatenate(parts)


def faces_of(field):
    got = []
    for dim, axis in enumerate(EVERY):
        size = field.shape[dim]
        low = lax.slice_in_dim(field, 0, 1, axis=dim)
        high = lax.slice_in_dim(field, size - 1, size, axis=dim)
        got.append(both_sides(low, high, axis))
    return got


def jacobi_step(field, faces, source):
    beside_all = source
    for dim in range(3):
        below, above = faces[dim]
        size = field.shape[dim]
        beside_all = beside_all + jnp.concatenate(
            [below, lax.slice_in_dim(field, 0, size - 1, axis=dim)], axis=dim
        )
        beside_all = beside_all + jnp.concatenate(
            [lax.slice_in_dim(field, 1, size, axis=dim), above], axis=dim
        )
    return beside_all / 6.0


def neighbour_numbers():
    counts = [lax.axis_size(axis) for axis in EVERY]
    here = [lax.axis_index(axis) for axis in EVERY]
    places = []
    for shift in (
        (0, 0, 0), (-1, 0, 0), (1, 0, 0), (0, -1, 0), (0, 1, 0), (0, 0, -1), (0, 0, 1)
    ):
        x, y, z = [(h + s + n) % n for h, s, n in zip(here, shift, counts)]
        places.append((x * counts[1] + y) * counts[2] + z)
    return jnp.stack(places)


def gather_plane(blocks):
    return lax.all_gather(blocks, PLANE, axis=0, tiled=True)


def scatter_plane(partial):
    return lax.psum_scatter(partial, PLANE, scatter_dimension=0, tiled=True)


def shards(
    ham_blocks, onsite, entry_slot, send_table, reads, gram_targets, table_pick, phi, potential_in
):
    plane = lax.axis_size(PLANE)
    held, width, _ = ham_blocks.shape
    lanes_count = send_table.shape[2]
    order = onsite.shape[1]
    side = order // width
    tables = phi.shape[1]
    points = phi.shape[3]
    slots = reads.shape[1]
    pairs = pairs_of(tables)

    gathered = gather_plane(ham_blocks)
    sent_numbers = plane * lanes_count
    numbers = jnp.concatenate([send_table.reshape(1, -1), table_pick.reshape(1, -1)], axis=1)
    numbers = lax.all_gather(numbers, EVERY, axis=0, tiled=True)
    mine = lax.axis_index(PLANE)
    owners = lax.axis_index("gx") * plane + jnp.arange(plane)
    theirs = jnp.take(numbers, owners, axis=0)[:, :sent_numbers]
    theirs = jnp.take(theirs.reshape(plane, plane, lanes_count), mine, axis=1)
    chosen = jnp.take(theirs.reshape(-1), entry_slot[0])
    bins = ((entry_slot[0] // lanes_count) * held + chosen).astype(jnp.int32)

    density = local_call(
        functools.partial(density_kernel, side),
        jax.ShapeDtypeStruct((side, width, width), jnp.bfloat16),
        [SMEM, VMEM, VMEM],
        [
            pltpu.VMEM((order, order), jnp.float32),
            pltpu.VMEM((order, order), jnp.bfloat16),
            pltpu.VMEM((order, order), jnp.bfloat16),
        ],
        flops=4 * order**3,
        moved=gathered.size * 2,
    )(bins, gathered, onsite)
    candidates = face_stack(density)
    first_faces = faces_of(potential_in)
    source = local_call(
        source_kernel,
        jax.ShapeDtypeStruct((points // 128, 128), jnp.float32),
        [SMEM, SMEM, VMEM, VMEM],
        [
            pltpu.VMEM((tables * tables, width, width), jnp.float32),
            pltpu.VMEM((tables * width, tables * width), jnp.bfloat16),
        ],
        flops=2 * points * (tables * width) ** 2,
        moved=phi.size * 2,
    )(reads[0], table_pick[0], candidates, phi[0]).reshape(potential_in.shape)
    potential = jacobi_step(potential_in, first_faces, source)
    potential = jacobi_step(potential, faces_of(potential), source)
    grams = local_call(
        gram_kernel,
        jax.ShapeDtypeStruct((len(pairs), width, width), jnp.bfloat16),
        [VMEM, VMEM],
        [pltpu.VMEM(((tables - 1) * width, (tables - 1) * width), jnp.float32)],
        flops=2 * points * (tables * width) ** 2,
        moved=phi.size * 2,
    )(phi[0], potential.reshape(points // 128, 128))
    gathered_grams = face_stack(grams)

    near = jnp.take(numbers, neighbour_numbers(), axis=0)[:, sent_numbers:]
    near = near.reshape(7, 2, slots)
    low = jnp.minimum(near[:, 0], near[:, 1])
    high = jnp.maximum(near[:, 0], near[:, 1])
    pair = low * tables - low * (low + 1) // 2 + high - low - 1
    column = (jnp.arange(7)[:, None] * len(pairs) + pair).reshape(-1).astype(jnp.int32)
    flip = (near[:, 0] > near[:, 1]).reshape(-1).astype(jnp.int32)
    padded = jnp.concatenate([bins, jnp.full((1,), plane * held, jnp.int32)])
    place = jnp.take(padded, gram_targets[0].reshape(-1))
    partial = local_call(
        combine_kernel,
        jax.ShapeDtypeStruct((plane * held, width, width), jnp.bfloat16),
        [SMEM, SMEM, SMEM, VMEM],
        [pltpu.VMEM((plane * held, width, width), jnp.float32)],
        flops=7 * slots * width * width,
        moved=plane * held * width * width * 2,
    )(place, column, flip, gathered_grams)
    grid_blocks = scatter_plane(partial).astype(jnp.float32)
    return (potential, grid_blocks)


def solution(mesh):
    placed = (
        P(EVERY, None, None),
        P(EVERY, None),
        P(EVERY, None),
        P(EVERY, None, None),
        P(EVERY, None),
        P(EVERY, None, None),
        P(EVERY, None, None),
        P(EVERY, None, None, None),
        P(*EVERY),
    )
    return jax.shard_map(
        shards,
        mesh=mesh,
        in_specs=placed,
        out_specs=(P(*EVERY), P(EVERY, None, None)),
        check_vma=False,
    )
```

time: 360 us -> 215 us (0.60)
  waiting for transfers between devices: 244 us -> 74 us
  blocking collectives: 0 us -> 68.2 us
  matrix products: 33.2 us -> 0 us
  local copies, waits for them, and re-layouts: 38.3 us -> 11.3 us
  Pallas kernels: 0 us -> 17.8 us
  between operations: 1.74 us -> 14.4 us
  starting transfers between devices: 34.7 us -> 23.8 us
    ppermute x24 -> x22, waiting for transfers between devices: 183 us -> 27.5 us  [the longest x12 20.7 us: both_sides(): below = lax.ppermute(high_part, axis, up)]
    all_gather x0 -> x1, blocking collectives: none -> 68.2 us  [shards(): numbers = lax.all_gather(numbers, EVERY, axis=0, tiled=True)]
    all_to_all x2 -> x0, waiting for transfers between devices: 61.4 us -> none  [the longest x1 31 us: shards(): lax.all_to_all(outgoing_back, ('gy', 'gz'), split_axis=0, concat_axis=0,...]
    reduce_scatter x0 -> x1, waiting for transfers between devices: none -> 46.4 us  [scatter_plane(): return lax.psum_scatter(partial, PLANE, scatter_dimension=0, tiled=True)]
    dot_general x6 -> x0, matrix products: 33.2 us -> none  [the longest x1 9.37 us: shards(): jnp.einsum('rij,rig->rjg', chosen_blocks, left_table, preferred_element_t...]
    pallas_call x0 -> x4, Pallas kernels: none -> 17.8 us  [the longest x1 5.71 us: shards(): local_call(combine_kernel, jax.ShapeDtypeStruct((plane * held, width, wid...]
    gather x5 -> x4, local copies, waits for them, and re-layouts: 15.9 us -> 2.66 us  [the longest x1 0.77 us: shards(): place = jnp.take(padded, gram_targets[0].reshape(-1))]
    all_to_all x2 -> x0, starting transfers between devices: 10 us -> none  [the longest x1 6.33 us: shards(): lax.all_to_all(outgoing, ('gy', 'gz'), split_axis=0, concat_axis=0, tiled...]
  transfers between devices with their start and end apart: 26 -> 24, of which waited for: 20 -> 15; matrix products, arithmetic and copies ran while one was open for 10% -> 4% of each run, Pallas kernels for 0% -> 4%
where the time goes in v1:
time: 215 us; the launch traced here: 214 us
  waiting for transfers between devices  74 us (34%)
  blocking collectives  68.2 us (32%)
  starting transfers between devices  23.8 us (11%)
  Pallas kernels  17.8 us (8%)
  between operations  14.4 us (7%)
  local copies, waits for them, and re-layouts  11.3 us (5%)
  other arithmetic  4.46 us (2%)
    all_gather x1, blocking collectives, shards(): numbers = lax.all_gather(numbers, EVERY, axis=0, tiled=True)  68.2 us
    reduce_scatter x1, waiting for transfers between devices, scatter_plane(): return lax.psum_scatter(partial, PLANE, scatter_dimension=0, tiled=True)  46.4 us
    ppermute x12, waiting for transfers between devices, both_sides(): below = lax.ppermute(high_part, axis, up)  20.7 us
    ppermute x10, starting transfers between devices, both_sides(): return (below, lax.ppermute(low_part, axis, down))  16.7 us
    ppermute x12, starting transfers between devices, both_sides(): below = lax.ppermute(high_part, axis, up)  6.95 us
    ppermute x10, waiting for transfers between devices, both_sides(): return (below, lax.ppermute(low_part, axis, down))  6.76 us
    pallas_call x1, Pallas kernels, shards(): local_call(combine_kernel, jax.ShapeDtypeStruct((plane * held, width, wid...  5.71 us
    unnamed x29, local copies, waits for them, and re-layouts  4.86 us
  transfers between devices with their start and end apart: 24, of which 15 were waited for; matrix products, arithmetic and copies ran while one was open for 4% of the time, Pallas kernels for 4%

profile of v1, /device:TPU:0, one launch (start us, length us, event | category | flops | bytes accessed | tf_op | source)
XLA Modules:
  0.0 213.8 jit_solution(17946932520198036413)
XLA Ops:
  7.2 0.7 fusion.31
  8.0 2.9 %collective-permute-start.5 = (f32[1,8,128]{2,1,0:T(8,128)S(1)}, f32[1,8,128]{2,1,0:T(8,128)S(1)}, u32[]{:S(2)}, u32[]{:S(2)}) collective-permute-start(f32[1,8,128]{2,1,0:T(8,128)S(1)} %get-tuple-element.41), channel_id=1, source_target_pairs={{0,8},{8,16},{16,24},{24,0},{1,9},{9,17},{17,25},{25,1},{2,10},{10... | collective-permute-start | bytes 12296 | tf_op jit(solution)/shard_map/ppermute | solution.py:170
  10.9 1.0 collective-permute-start.6
  11.9 0.8 fusion.29
  12.7 0.7 reduce.1
  13.6 0.8 reshape.448
  14.4 0.8 copy.20
  15.2 0.1 stack.55
  15.4 68.2 %all-gather = s32[32,1,56]{2,1,0:T(1,128)S(1)} all-gather(s32[1,1,56]{2,1,0:T(1,128)S(1)} %add_bitcast_fusion), channel_id=1, replica_groups=mesh['gx'=4,'gy'=2,'gz'=4] {'gx','gy','gz'}, dimensions={0}, use_global_device_ids=true | all-gather | bytes 7392 | tf_op jit(solution)/shard_map/all_gather | solution.py:243
  83.6 0.6 gather_fusion
  84.6 0.6 gather_fusion.3
  85.7 0.7 fusion.17
  86.4 0.8 gather_fusion.1
  87.4 1.6 copy-done.2
  89.0 4.4 %shard_map.104 = bf16[6,128,128]{2,1,0:T(8,128)(2,1)S(1)} custom-call(s32[36]{0:T(128)S(1)} %fusion.15.bins_ref, bf16[64,128,128]{2,1,0:T(8,128)(2,1)S(1)} %copy-done.2, f32[1,768]{1,0:T(1,128)S(1)} %copy-done.3), custom_call_target="tpu_custom_call" | custom-call | flops 1811939328 | bytes 2097152 | tf_op jit(solution)/shard_map/pallas_call | solution.py:251
  93.6 0.8 gather_fusion.2
  94.4 3.0 %collective-permute-start.1 = (bf16[6,128,128]{2,1,0:T(8,128)(2,1)S(1)}, bf16[6,128,128]{2,1,0:T(8,128)(2,1)S(1)}, u32[]{:S(2)}, u32[]{:S(2)}) collective-permute-start(bf16[6,128,128]{2,1,0:T(8,128)(2,1)S(1)} %shard_map.104), channel_id=1, source_target_pairs={{8,0},{16,8},{24,16},{0,24},{9,1},{17,9},{25,17},{1,25},{10,2},{18... | collective-permute-start | bytes 589832 | tf_op jit(solution)/shard_map/ppermute | solution.py:173
  97.4 2.7 %collective-permute-done = bf16[6,128,128]{2,1,0:T(8,128)(2,1)S(1)} collective-permute-done((bf16[6,128,128]{2,1,0:T(8,128)(2,1)S(1)}, bf16[6,128,128]{2,1,0:T(8,128)(2,1)S(1)}, u32[]{:S(2)}, u32[]{:S(2)}) %collective-permute-start) | collective-permute-done | bytes 196640 | tf_op jit(solution)/shard_map/ppermute | solution.py:170
  100.1 1.0 collective-permute-done.1
  101.2 0.3 collective-permute-done.2
  101.5 3.5 %collective-permute-start.4 = (bf16[6,128,128]{2,1,0:T(8,128)(2,1)S(1)}, bf16[6,128,128]{2,1,0:T(8,128)(2,1)S(1)}, u32[]{:S(2)}, u32[]{:S(2)}) collective-permute-start(bf16[6,128,128]{2,1,0:T(8,128)(2,1)S(1)} %shard_map.104), channel_id=1, source_target_pairs={{1,0},{2,1},{3,2},{0,3},{5,4},{6,5},{7,6},{4,7},{9,8},{10,9},{11,1... | collective-permute-start | bytes 589832 | tf_op jit(solution)/shard_map/ppermute | solution.py:173
  105.1 5.7 %collective-permute-done.3 = bf16[6,128,128]{2,1,0:T(8,128)(2,1)S(1)} collective-permute-done((bf16[6,128,128]{2,1,0:T(8,128)(2,1)S(1)}, bf16[6,128,128]{2,1,0:T(8,128)(2,1)S(1)}, u32[]{:S(2)}, u32[]{:S(2)}) %collective-permute-start.3) | collective-permute-done | bytes 196640 | tf_op jit(solution)/shard_map/ppermute | solution.py:170
  110.8 1.9 collective-permute-done.4
  112.7 5.5 %collective-permute-done.9 = f32[4,8,1]{2,1,0:T(8,128)S(1)} collective-permute-done((f32[4,8,1]{2,1,0:T(8,128)S(1)}, f32[4,8,1]{2,1,0:T(8,128)S(1)}, u32[]{:S(2)}, u32[]{:S(2)}) %collective-permute-start.9) | collective-permute-done | bytes 160 | tf_op jit(solution)/shard_map/ppermute | solution.py:170
  118.2 2.2 %copy-done = bf16[1,4,128,4096]{3,2,1,0:T(8,128)(2,1)S(1)} copy-done((bf16[1,4,128,4096]{3,2,1,0:T(8,128)(2,1)S(1)}, bf16[1,4,128,4096]{3,2,1,0:T(8,128)(2,1)}, u32[]{:S(2)}) %copy-start) | copy-done | bytes 4194328
  120.4 4.4 %shard_map.105 = f32[32,128]{1,0:T(8,128)S(1)} custom-call(s32[8]{0:T(128)S(1)} %bitcast.80, s32[2,8]{1,0:T(2,128)S(1)} %bitcast.79, bf16[42,128,128]{2,1,0:T(8,128)(2,1)S(1)} %constant_dynamic-update-slice_fusion.blocks_ref, bf16[4,128,4096]{2,1,0:T(8,128)(2,1)S(1)} %bitcast.77), custom_call_target="tpu_custom_call" | custom-call | flops 2147483648 | bytes 4194304 | tf_op jit(solution)/shard_map/pallas_call | solution.py:265
  124.8 0.1 fusion.5
  125.1 2.1 collective-permute-start.15
  127.2 1.8 collective-permute-start.16
  129.0 0.9 collective-permute-start.12
  129.9 1.1 collective-permute-start.11
  131.0 0.5 collective-permute-start.13
  131.5 0.6 collective-permute-done.14
  132.2 0.2 collective-permute-done.13
  132.3 0.2 collective-permute-done.12
  132.6 1.8 collective-permute-done.11
  134.5 3.2 %shard_map.106 = bf16[6,128,128]{2,1,0:T(8,128)(2,1)S(1)} custom-call(bf16[4,128,4096]{2,1,0:T(8,128)(2,1)S(1)} %bitcast.78, f32[32,128]{1,0:T(8,128)S(1)} %fusion.9.v_ref), custom_call_target="tpu_custom_call" | custom-call | flops 2147483648 | bytes 4194304 | tf_op jit(solution)/shard_map/pallas_call | solution.py:278
  137.7 0.3 collective-permute-start.17
  138.1 2.7 %collective-permute-start.18 = (bf16[6,128,128]{2,1,0:T(8,128)(2,1)S(1)}, bf16[6,128,128]{2,1,0:T(8,128)(2,1)S(1)}, u32[]{:S(2)}, u32[]{:S(2)}) collective-permute-start(bf16[6,128,128]{2,1,0:T(8,128)(2,1)S(1)} %shard_map.106), channel_id=1, source_target_pairs={{8,0},{16,8},{24,16},{0,24},{9,1},{17,9},{25,17},{1,25},{10,2},{18... | collective-permute-start | bytes 589832 | tf_op jit(solution)/shard_map/ppermute | solution.py:173
  140.8 3.8 %collective-permute-start.21 = (bf16[6,128,128]{2,1,0:T(8,128)(2,1)S(1)}, bf16[6,128,128]{2,1,0:T(8,128)(2,1)S(1)}, u32[]{:S(2)}, u32[]{:S(2)}) collective-permute-start(bf16[6,128,128]{2,1,0:T(8,128)(2,1)S(1)} %shard_map.106), channel_id=1, source_target_pairs={{1,0},{2,1},{3,2},{0,3},{5,4},{6,5},{7,6},{4,7},{9,8},{10,9},{11,1... | collective-permute-start | bytes 589832 | tf_op jit(solution)/shard_map/ppermute | solution.py:173
  144.7 1.2 collective-permute-done.17
  145.9 1.0 collective-permute-done.18
  147.1 3.3 %collective-permute-done.20 = bf16[6,128,128]{2,1,0:T(8,128)(2,1)S(1)} collective-permute-done((bf16[6,128,128]{2,1,0:T(8,128)(2,1)S(1)}, bf16[6,128,128]{2,1,0:T(8,128)(2,1)S(1)}, u32[]{:S(2)}, u32[]{:S(2)}) %collective-permute-start.20) | collective-permute-done | bytes 196640 | tf_op jit(solution)/shard_map/ppermute | solution.py:170
  150.4 2.0 collective-permute-done.21
  152.4 5.7 %shard_map.107 = bf16[64,128,128]{2,1,0:T(8,128)(2,1)} custom-call(s32[56]{0:T(128)S(1)} %and_select_fusion.1.bin_ref, s32[56]{0:T(128)S(1)} %add_add_fusion.col_ref, s32[56]{0:T(128)S(1)} %reshape.482.flip_ref, bf16[42,128,128]{2,1,0:T(8,128)(2,1)S(1)} %constant_dynamic-update-slice_fusion.7.blocks_ref), custom_call_target="tpu_custom_call" | custom-call | flops 917504 | bytes 2097152 | tf_op jit(solution)/shard_map/pallas_call | solution.py:297
  158.1 0.7 fusion.7
  158.8 46.4 %reduce-scatter.2.cloned.1.call-done = bf16[8,128,128]{2,1,0:T(8,128)(2,1)} async-done(((bf16[64,128,128]{2,1,0:T(8,128)(2,1)}), bf16[8,128,128]{2,1,0:T(8,128)(2,1)}) %reduce-scatter.2.cloned.1.call-update) | async-done | bytes 262160 | tf_op jit(solution)/shard_map/reduce_scatter | solution.py:224
  205.2 1.8 convert_element_type.10
  (92 shorter events, 2.5 us)
Async XLA Ops:
  7.2 80.0 %copy-start.6 = (f32[4,8,128]{2,1,0:T(8,128)S(1)}, f32[4,8,128]{2,1,0:T(8,128)}, u32[]{:S(2)}) copy-start(f32[4,8,128]{2,1,0:T(8,128)} %param.17) | copy-start | bytes 49156
  7.2 80.0 %copy-start.7 = (s32[1,36]{1,0:T(1,128)S(1)}, s32[1,36]{1,0:T(1,128)}, u32[]{:S(2)}) copy-start(s32[1,36]{1,0:T(1,128)} %param.11) | copy-start | bytes 436
  7.2 80.2 %copy-start.3 = (f32[1,768]{1,0:T(1,128)S(1)}, f32[1,768]{1,0:T(1,128)}, u32[]{:S(2)}) copy-start(f32[1,768]{1,0:T(1,128)} %onsite_ref.1) | copy-start | bytes 9220
  7.2 80.2 %all-gather.3.cloned.1.call-start = ((), (), s32[]{:S(2)}) async-start(), calls=%async_computation.1 | async-start | bytes 2359296 | tf_op jit(solution)/shard_map/all_gather | solution.py:220
  8.0 116.9 %collective-permute-start.5 = (f32[1,8,128]{2,1,0:T(8,128)S(1)}, f32[1,8,128]{2,1,0:T(8,128)S(1)}, u32[]{:S(2)}, u32[]{:S(2)}) collective-permute-start(f32[1,8,128]{2,1,0:T(8,128)S(1)} %get-tuple-element.41), channel_id=1, source_target_pairs={{0,8},{8,16},{16,24},{24,0},{1,9},{9,17},{17,25},{25,1},{2,10},{10... | collective-permute-start | bytes 12296 | tf_op jit(solution)/shard_map/ppermute | solution.py:170
  10.9 113.9 %collective-permute-start.6 = (f32[1,8,128]{2,1,0:T(8,128)S(1)}, f32[1,8,128]{2,1,0:T(8,128)S(1)}, u32[]{:S(2)}, u32[]{:S(2)}) collective-permute-start(f32[1,8,128]{2,1,0:T(8,128)S(1)} %get-tuple-element.40), channel_id=1, source_target_pairs={{8,0},{16,8},{24,16},{0,24},{9,1},{17,9},{25,17},{1,25},{10,2},{18... | collective-permute-start | bytes 12296 | tf_op jit(solution)/shard_map/ppermute | solution.py:173
  11.9 193.3 %reduce-scatter.2.cloned.1.call-start = ((), (), s32[]{:S(2)}) async-start(), calls=%async_computation.2 | async-start | bytes 2359296 | tf_op jit(solution)/shard_map/reduce_scatter | solution.py:224
  12.7 112.1 %collective-permute-start.7 = (f32[4,1,128]{2,1,0:T(1,128)S(1)}, f32[4,1,128]{2,1,0:T(1,128)S(1)}, u32[]{:S(2)}, u32[]{:S(2)}) collective-permute-start(f32[4,1,128]{2,1,0:T(1,128)S(1)} %get-tuple-element.37), channel_id=1, source_target_pairs={{0,4},{4,0},{1,5},{5,1},{2,6},{6,2},{3,7},{7,3},{8,12},{12,8},{9,1... | collective-permute-start | bytes 6152 | tf_op jit(solution)/shard_map/ppermute | solution.py:170
  87.4 1.6 copy-start.2
  93.4 6.6 %collective-permute-start = (bf16[6,128,128]{2,1,0:T(8,128)(2,1)S(1)}, bf16[6,128,128]{2,1,0:T(8,128)(2,1)S(1)}, u32[]{:S(2)}, u32[]{:S(2)}) collective-permute-start(bf16[6,128,128]{2,1,0:T(8,128)(2,1)S(1)} %shard_map.104), channel_id=1, source_target_pairs={{0,8},{8,16},{16,24},{24,0},{1,9},{9,17},{17,25},{25,1},{2,10},{10... | collective-permute-start | bytes 589832 | tf_op jit(solution)/shard_map/ppermute | solution.py:170
  94.4 23.9 %copy-start.4 = (s32[1,2,8]{2,1,0:T(2,128)S(1)}, s32[1,2,8]{2,1,0:T(2,128)}, u32[]{:S(2)}) copy-start(s32[1,2,8]{2,1,0:T(2,128)} %param.15) | copy-start | bytes 196
  94.4 23.8 %copy-start.5 = (s32[1,8]{1,0:T(1,128)S(1)}, s32[1,8]{1,0:T(1,128)}, u32[]{:S(2)}) copy-start(s32[1,8]{1,0:T(1,128)} %param.13) | copy-start | bytes 100
  94.4 6.8 %collective-permute-start.1 = (bf16[6,128,128]{2,1,0:T(8,128)(2,1)S(1)}, bf16[6,128,128]{2,1,0:T(8,128)(2,1)S(1)}, u32[]{:S(2)}, u32[]{:S(2)}) collective-permute-start(bf16[6,128,128]{2,1,0:T(8,128)(2,1)S(1)} %shard_map.104), channel_id=1, source_target_pairs={{8,0},{16,8},{24,16},{0,24},{9,1},{17,9},{25,17},{1,25},{10,2},{18... | collective-permute-start | bytes 589832 | tf_op jit(solution)/shard_map/ppermute | solution.py:173
  100.1 1.4 collective-permute-start.2
  101.1 9.6 %collective-permute-start.3 = (bf16[6,128,128]{2,1,0:T(8,128)(2,1)S(1)}, bf16[6,128,128]{2,1,0:T(8,128)(2,1)S(1)}, u32[]{:S(2)}, u32[]{:S(2)}) collective-permute-start(bf16[6,128,128]{2,1,0:T(8,128)(2,1)S(1)} %shard_map.104), channel_id=1, source_target_pairs={{0,1},{1,2},{2,3},{3,0},{4,5},{5,6},{6,7},{7,4},{8,9},{9,10},{10,1... | collective-permute-start | bytes 589832 | tf_op jit(solution)/shard_map/ppermute | solution.py:170
  101.5 11.2 %collective-permute-start.4 = (bf16[6,128,128]{2,1,0:T(8,128)(2,1)S(1)}, bf16[6,128,128]{2,1,0:T(8,128)(2,1)S(1)}, u32[]{:S(2)}, u32[]{:S(2)}) collective-permute-start(bf16[6,128,128]{2,1,0:T(8,128)(2,1)S(1)} %shard_map.104), channel_id=1, source_target_pairs={{1,0},{2,1},{3,2},{0,3},{5,4},{6,5},{7,6},{4,7},{9,8},{10,9},{11,1... | collective-permute-start | bytes 589832 | tf_op jit(solution)/shard_map/ppermute | solution.py:173
  110.8 14.1 %collective-permute-start.8 = (f32[4,1,128]{2,1,0:T(1,128)S(1)}, f32[4,1,128]{2,1,0:T(1,128)S(1)}, u32[]{:S(2)}, u32[]{:S(2)}) collective-permute-start(f32[4,1,128]{2,1,0:T(1,128)S(1)} %get-tuple-element.36), channel_id=1, source_target_pairs={{4,0},{0,4},{5,1},{1,5},{6,2},{2,6},{7,3},{3,7},{12,8},{8,12},{13,... | collective-permute-start | bytes 6152 | tf_op jit(solution)/shard_map/ppermute | solution.py:173
  112.7 5.5 %collective-permute-start.9 = (f32[4,8,1]{2,1,0:T(8,128)S(1)}, f32[4,8,1]{2,1,0:T(8,128)S(1)}, u32[]{:S(2)}, u32[]{:S(2)}) collective-permute-start(f32[4,8,1]{2,1,0:T(8,128)S(1)} %get-tuple-element.33), channel_id=1, source_target_pairs={{0,1},{1,2},{2,3},{3,0},{4,5},{5,6},{6,7},{7,4},{8,9},{9,10},{10,1... | collective-permute-start | bytes 392 | tf_op jit(solution)/shard_map/ppermute | solution.py:170
  118.2 6.6 %collective-permute-start.10 = (f32[4,8,1]{2,1,0:T(8,128)S(1)}, f32[4,8,1]{2,1,0:T(8,128)S(1)}, u32[]{:S(2)}, u32[]{:S(2)}) collective-permute-start(f32[4,8,1]{2,1,0:T(8,128)S(1)} %get-tuple-element.32), channel_id=1, source_target_pairs={{1,0},{2,1},{3,2},{0,3},{5,4},{6,5},{7,6},{4,7},{9,8},{10,9},{11,1... | collective-permute-start | bytes 392 | tf_op jit(solution)/shard_map/ppermute | solution.py:173
  118.2 2.2 %copy-start = (bf16[1,4,128,4096]{3,2,1,0:T(8,128)(2,1)S(1)}, bf16[1,4,128,4096]{3,2,1,0:T(8,128)(2,1)}, u32[]{:S(2)}) copy-start(bf16[1,4,128,4096]{3,2,1,0:T(8,128)(2,1)} %param.16) | copy-start | bytes 12582916
  120.4 14.1 %copy-start.1 = (bf16[1,4,128,4096]{3,2,1,0:T(8,128)(2,1)S(1)}, bf16[1,4,128,4096]{3,2,1,0:T(8,128)(2,1)}, u32[]{:S(2)}) copy-start(bf16[1,4,128,4096]{3,2,1,0:T(8,128)(2,1)} %param.16) | copy-start | bytes 12582916
  125.1 5.9 %collective-permute-start.15 = (f32[4,8,1]{2,1,0:T(8,128)S(1)}, f32[4,8,1]{2,1,0:T(8,128)S(1)}, u32[]{:S(2)}, u32[]{:S(2)}) collective-permute-start(f32[4,8,1]{2,1,0:T(8,128)S(1)} %get-tuple-element.29), channel_id=1, source_target_pairs={{0,1},{1,2},{2,3},{3,0},{4,5},{5,6},{6,7},{7,4},{8,9},{9,10},{10,1... | collective-permute-start | bytes 392 | tf_op jit(solution)/shard_map/ppermute | solution.py:170
  127.2 4.4 %collective-permute-start.16 = (f32[4,8,1]{2,1,0:T(8,128)S(1)}, f32[4,8,1]{2,1,0:T(8,128)S(1)}, u32[]{:S(2)}, u32[]{:S(2)}) collective-permute-start(f32[4,8,1]{2,1,0:T(8,128)S(1)} %get-tuple-element.28), channel_id=1, source_target_pairs={{1,0},{2,1},{3,2},{0,3},{5,4},{6,5},{7,6},{4,7},{9,8},{10,9},{11,1... | collective-permute-start | bytes 392 | tf_op jit(solution)/shard_map/ppermute | solution.py:173
  129.0 3.6 %collective-permute-start.12 = (f32[1,8,128]{2,1,0:T(8,128)S(1)}, f32[1,8,128]{2,1,0:T(8,128)S(1)}, u32[]{:S(2)}, u32[]{:S(2)}) collective-permute-start(f32[1,8,128]{2,1,0:T(8,128)S(1)} %get-tuple-element.25), channel_id=1, source_target_pairs={{8,0},{16,8},{24,16},{0,24},{9,1},{17,9},{25,17},{1,25},{10,2},{18... | collective-permute-start | bytes 12296 | tf_op jit(solution)/shard_map/ppermute | solution.py:173
  129.9 4.5 %collective-permute-start.11 = (f32[1,8,128]{2,1,0:T(8,128)S(1)}, f32[1,8,128]{2,1,0:T(8,128)S(1)}, u32[]{:S(2)}, u32[]{:S(2)}) collective-permute-start(f32[1,8,128]{2,1,0:T(8,128)S(1)} %get-tuple-element.24), channel_id=1, source_target_pairs={{0,8},{8,16},{16,24},{24,0},{1,9},{9,17},{17,25},{25,1},{2,10},{10... | collective-permute-start | bytes 12296 | tf_op jit(solution)/shard_map/ppermute | solution.py:170
  131.0 1.2 collective-permute-start.14
  131.0 1.3 collective-permute-start.13
  137.7 8.2 %collective-permute-start.17 = (bf16[6,128,128]{2,1,0:T(8,128)(2,1)S(1)}, bf16[6,128,128]{2,1,0:T(8,128)(2,1)S(1)}, u32[]{:S(2)}, u32[]{:S(2)}) collective-permute-start(bf16[6,128,128]{2,1,0:T(8,128)(2,1)S(1)} %shard_map.106), channel_id=1, source_target_pairs={{0,8},{8,16},{16,24},{24,0},{1,9},{9,17},{17,25},{25,1},{2,10},{10... | collective-permute-start | bytes 589832 | tf_op jit(solution)/shard_map/ppermute | solution.py:170
  138.1 8.9 %collective-permute-start.18 = (bf16[6,128,128]{2,1,0:T(8,128)(2,1)S(1)}, bf16[6,128,128]{2,1,0:T(8,128)(2,1)S(1)}, u32[]{:S(2)}, u32[]{:S(2)}) collective-permute-start(bf16[6,128,128]{2,1,0:T(8,128)(2,1)S(1)} %shard_map.106), channel_id=1, source_target_pairs={{8,0},{16,8},{24,16},{0,24},{9,1},{17,9},{25,17},{1,25},{10,2},{18... | collective-permute-start | bytes 589832 | tf_op jit(solution)/shard_map/ppermute | solution.py:173
  140.8 6.2 %collective-permute-start.19 = (bf16[6,128,128]{2,1,0:T(8,128)(2,1)S(1)}, bf16[6,128,128]{2,1,0:T(8,128)(2,1)S(1)}, u32[]{:S(2)}, u32[]{:S(2)}) collective-permute-start(bf16[6,128,128]{2,1,0:T(8,128)(2,1)S(1)} %shard_map.106), channel_id=1, source_target_pairs={{0,4},{4,0},{1,5},{5,1},{2,6},{6,2},{3,7},{7,3},{8,12},{12,8},{9,1... | collective-permute-start | bytes 589832 | tf_op jit(solution)/shard_map/ppermute | solution.py:170
  140.8 9.5 %collective-permute-start.20 = (bf16[6,128,128]{2,1,0:T(8,128)(2,1)S(1)}, bf16[6,128,128]{2,1,0:T(8,128)(2,1)S(1)}, u32[]{:S(2)}, u32[]{:S(2)}) collective-permute-start(bf16[6,128,128]{2,1,0:T(8,128)(2,1)S(1)} %shard_map.106), channel_id=1, source_target_pairs={{0,1},{1,2},{2,3},{3,0},{4,5},{5,6},{6,7},{7,4},{8,9},{9,10},{10,1... | collective-permute-start | bytes 589832 | tf_op jit(solution)/shard_map/ppermute | solution.py:170
  140.8 11.5 %collective-permute-start.21 = (bf16[6,128,128]{2,1,0:T(8,128)(2,1)S(1)}, bf16[6,128,128]{2,1,0:T(8,128)(2,1)S(1)}, u32[]{:S(2)}, u32[]{:S(2)}) collective-permute-start(bf16[6,128,128]{2,1,0:T(8,128)(2,1)S(1)} %shard_map.106), channel_id=1, source_target_pairs={{1,0},{2,1},{3,2},{0,3},{5,4},{6,5},{7,6},{4,7},{9,8},{10,9},{11,1... | collective-permute-start | bytes 589832 | tf_op jit(solution)/shard_map/ppermute | solution.py:173
Sparse Core Ops, SparseCore 0:
  12.0 30.0 all-gather.2
  158.2 46.9 reduce-scatter.1

commit v2 on v1

--- a/solution.py
+++ b/solution.py
@@ -13,6 +13,7 @@
 VMEM_LIMIT = 48 * 1024 * 1024
 VMEM = pl.BlockSpec(memory_space=pltpu.VMEM)
 SMEM = pl.BlockSpec(memory_space=pltpu.SMEM)
+MESH = pl.DeviceIdType.MESH
 
 
 def local_call(kernel, out_shape, in_specs, scratch=(), flops=0, moved=0):
@@ -205,23 +206,342 @@
 
 
 def neighbour_numbers():
-    counts = [lax.axis_size(axis) for axis in EVERY]
-    here = [lax.axis_index(axis) for axis in EVERY]
+    rows, line = lax.axis_size("gy"), lax.axis_size("gz")
+    row, z = lax.axis_index("gy"), lax.axis_index("gz")
     places = []
-    for shift in (
-        (0, 0, 0), (-1, 0, 0), (1, 0, 0), (0, -1, 0), (0, 1, 0), (0, 0, -1), (0, 0, 1)
-    ):
-        x, y, z = [(h + s + n) % n for h, s, n in zip(here, shift, counts)]
-        places.append((x * counts[1] + y) * counts[2] + z)
+    for i, k in ((-1, 0), (1, 0), (0, -1), (0, 1)):
+        places.append((row + i + rows) % rows * line + (z + k + line) % line)
     return jnp.stack(places)
 
 
-def gather_plane(blocks):
-    return lax.all_gather(blocks, PLANE, axis=0, tiled=True)
+def greet_plane(line, group, z, row):
+    barrier = pltpu.get_barrier_semaphore()
+
+    @pl.when(z > 0)
+    def _():
+        pl.semaphore_signal(barrier, inc=1, device_id={"gz": z - 1}, device_id_type=MESH)
+
+    @pl.when(z < line - 1)
+    def _():
+        pl.semaphore_signal(barrier, inc=1, device_id={"gz": z + 1}, device_id_type=MESH)
+
+    for j in range(1, group):
+        pl.semaphore_signal(
+            barrier, inc=1, device_id={"gy": lax.rem(row + j, group)}, device_id_type=MESH
+        )
+
+    below = lax.div(z + line - 1, line)
+    above = lax.div(2 * line - 2 - z, line)
+    pl.semaphore_wait(barrier, group - 1 + below + above)
+
+
+def pieces_of(count):
+    return 4 if count % 4 == 0 else 1
+
+
+def gather_kernel(
+    line, group, x_ref, n_ref, out_ref, nout_ref, line_send, line_recv, row_send, row_recv
+):
+    z, row = lax.axis_index("gz"), lax.axis_index("gy")
+    held, tall = x_ref.shape[0], n_ref.shape[0]
+    pieces = pieces_of(held)
+    part = held // pieces
+
+    def slot(owner_row, owner_z, c):
+        owner = owner_row * line + owner_z
+        if c < pieces:
+            return out_ref.at[pl.ds(owner * held + c * part, part)]
+        return nout_ref.at[pl.ds(pl.multiple_of(owner * tall, tall), tall)]
+
+    def source(c):
+        return x_ref.at[pl.ds(c * part, part)] if c < pieces else n_ref
+
+    def along(origin, c, side, own):
+        return pltpu.make_async_remote_copy(
+            src_ref=source(c) if own else slot(row, origin, c),
+            dst_ref=slot(row, origin, c),
+            send_sem=line_send.at[side, origin, c],
+            recv_sem=line_recv.at[origin, c],
+            device_id={"gz": z + 1 if side == 0 else z - 1},
+            device_id_type=MESH,
+        )
+
+    def across(j, origin, kind, own):
+        owner = row * line + origin
+        if kind == 0:
+            dst = out_ref.at[pl.ds(owner * held, held)]
+            src = x_ref if own else dst
+        else:
+            dst = nout_ref.at[pl.ds(pl.multiple_of(owner * tall, tall), tall)]
+            src = n_ref if own else dst
+        return pltpu.make_async_remote_copy(
+            src_ref=src,
+            dst_ref=dst,
+            send_sem=row_send.at[j - 1, origin, kind],
+            recv_sem=row_recv.at[j - 1, origin, kind],
+            device_id={"gy": lax.rem(row + j, group)},
+            device_id_type=MESH,
+        )
+
+    def arrived(j, origin, kind):
+        owner = lax.rem(row + group - j, group) * line + origin
+        if kind == 0:
+            dst = out_ref.at[pl.ds(owner * held, held)]
+        else:
+            dst = nout_ref.at[pl.ds(pl.multiple_of(owner * tall, tall), tall)]
+        return pltpu.make_async_remote_copy(
+            src_ref=dst,
+            dst_ref=dst,
+            send_sem=row_send.at[j - 1, origin, kind],
+            recv_sem=row_recv.at[j - 1, origin, kind],
+            device_id={"gy": lax.rem(row + j, group)},
+            device_id_type=MESH,
+        )
+
+    greet_plane(line, group, z, row)
+    order = [pieces] + list(range(pieces))
+    for c in order:
+
+        @pl.when(z < line - 1)
+        def _():
+            along(z, c, 0, True).start()
+
+        @pl.when(z > 0)
+        def _():
+            along(z, c, 1, True).start()
+
+    for j in range(1, group):
+        for kind in range(2):
+            across(j, z, kind, True).start()
+    mine = row * line + z
+    out_ref[pl.ds(mine * held, held)] = x_ref[...]
+    nout_ref[pl.ds(pl.multiple_of(mine * tall, tall), tall), :] = n_ref[...]
+    for s in range(1, line):
+        for c in order:
+
+            @pl.when(z >= s)
+            def _():
+                along(z - s, c, 0, False).wait_recv()
+
+            @pl.when((z >= s) & (z < line - 1))
+            def _():
+                along(z - s, c, 0, False).start()
+
+            @pl.when(z + s < line)
+            def _():
+                along(z + s, c, 1, False).wait_recv()
+
+            @pl.when((z + s < line) & (z > 0))
+            def _():
+                along(z + s, c, 1, False).start()
+
+        for j in range(1, group):
+            for kind in range(2):
+
+                @pl.when(z >= s)
+                def _():
+                    across(j, z - s, kind, False).start()
+
+                @pl.when(z + s < line)
+                def _():
+                    across(j, z + s, kind, False).start()
+
+    for j in range(1, group):
+        for origin in range(line):
+            for kind in range(2):
+                arrived(j, origin, kind).wait_recv()
+                across(j, origin, kind, False).wait_send()
+    for s in range(line):
+        for c in order:
+
+            @pl.when((z >= s) & (z < line - 1))
+            def _():
+                along(z - s, c, 0, False).wait_send()
+
+            @pl.when((z + s < line) & (z > 0))
+            def _():
+                along(z + s, c, 1, False).wait_send()
+
+
+def gather_plane(blocks, numbers):
+    line, group = lax.axis_size("gz"), lax.axis_size("gy")
+    plane = line * group
+    kinds = pieces_of(blocks.shape[0]) + 1
+    others = max(group - 1, 1)
+    return pl.pallas_call(
+        functools.partial(gather_kernel, line, group),
+        out_shape=(
+            jax.ShapeDtypeStruct((plane * blocks.shape[0],) + blocks.shape[1:], blocks.dtype),
+            jax.ShapeDtypeStruct((plane * numbers.shape[0], numbers.shape[1]), numbers.dtype),
+        ),
+        in_specs=[VMEM, VMEM],
+        out_specs=(VMEM, VMEM),
+        scratch_shapes=[
+            pltpu.SemaphoreType.DMA((2, line, kinds)),
+            pltpu.SemaphoreType.DMA((line, kinds)),
+            pltpu.SemaphoreType.DMA((others, line, 2)),
+            pltpu.SemaphoreType.DMA((others, line, 2)),
+        ],
+        compiler_params=pltpu.CompilerParams(
+            collective_id=1, has_side_effects=True, vmem_limit_bytes=VMEM_LIMIT
+        ),
+    )(blocks, numbers)
+
+
+def scatter_kernel(
+    line, group, x_ref, out_ref, row_buf, acc_buf, pass_buf,
+    row_send, row_recv, line_send, line_recv,
+):
+    z, row = lax.axis_index("gz"), lax.axis_index("gy")
+    held = out_ref.shape[0]
+    pieces = pieces_of(held)
+    part = held // pieces
+    f32 = jnp.float32
+
+    def across(j, target):
+        peer = lax.rem(row + j, group)
+        return pltpu.make_async_remote_copy(
+            src_ref=x_ref.at[pl.ds((peer * line + target) * held, held)],
+            dst_ref=row_buf.at[j - 1, target],
+            send_sem=row_send.at[j - 1, target],
+            recv_sem=row_recv.at[j - 1, target],
+            device_id={"gy": peer},
+            device_id_type=MESH,
+        )
+
+    def along(side, target, c):
+        piece = pass_buf.at[side, target, pl.ds(c * part, part)]
+        return pltpu.make_async_remote_copy(
+            src_ref=piece,
+            dst_ref=piece,
+            send_sem=line_send.at[side, target, c],
+            recv_sem=line_recv.at[side, target, c],
+            device_id={"gz": z + 1 if side == 0 else z - 1},
+            device_id_type=MESH,
+        )
+
+    greet_plane(line, group, z, row)
+    turn = []
+    for k in range((line + 1) // 2):
+        turn.extend({line - 1 - k: 0, k: 0})
+    for target in turn:
+        for j in range(1, group):
+            across(j, target).start()
+
+    def gathered(target):
+        for j in range(1, group):
+            across(j, target).wait_recv()
+        total = x_ref[pl.ds((row * line + target) * held, held)].astype(f32)
+        for j in range(1, group):
+            total = total + row_buf[j - 1, target].astype(f32)
+        acc_buf[target] = total.astype(acc_buf.dtype)
+
+    for target in turn:
+        gathered(target)
+        if target == line - 1:
+            @pl.when(z == 0)
+            def _():
+                for c in range(pieces):
+                    pass_buf[0, target, pl.ds(c * part, part)] = acc_buf[
+                        target, pl.ds(c * part, part)
+                    ]
+                    along(0, target, c).start()
+
+        if target == 0:
+            @pl.when(z == line - 1)
+            def _():
+                for c in range(pieces):
+                    pass_buf[1, target, pl.ds(c * part, part)] = acc_buf[
+                        target, pl.ds(c * part, part)
+                    ]
+                    along(1, target, c).start()
+
+    for k in range(line - 1):
+        high, low = line - 1 - k, k
+        for c in range(pieces):
+            here = pl.ds(c * part, part)
+            if high != line - 1:
+                @pl.when((z == 0) & (high > z))
+                def _():
+                    pass_buf[0, high, here] = acc_buf[high, here]
+                    along(0, high, c).start()
+
+            @pl.when((z > 0) & (high > z))
+            def _():
+                along(0, high, c).wait_recv()
+                pass_buf[0, high, here] = (
+                    pass_buf[0, high, here].astype(f32) + acc_buf[high, here].astype(f32)
+                ).astype(acc_buf.dtype)
+                along(0, high, c).start()
+
+            if low != 0:
+                @pl.when((z == line - 1) & (low < z))
+                def _():
+                    pass_buf[1, low, here] = acc_buf[low, here]
+                    along(1, low, c).start()
+
+            @pl.when((z < line - 1) & (low < z))
+            def _():
+                along(1, low, c).wait_recv()
+                pass_buf[1, low, here] = (
+                    pass_buf[1, low, here].astype(f32) + acc_buf[low, here].astype(f32)
+                ).astype(acc_buf.dtype)
+                along(1, low, c).start()
+
+    out_ref[...] = acc_buf[z].astype(f32)
+
+    @pl.when(z > 0)
+    def _():
+        for c in range(pieces):
+            here = pl.ds(c * part, part)
+            along(0, z, c).wait_recv()
+            out_ref[here] = out_ref[here] + pass_buf[0, z, here].astype(f32)
+
+    @pl.when(z < line - 1)
+    def _():
+        for c in range(pieces):
+            here = pl.ds(c * part, part)
+            along(1, z, c).wait_recv()
+            out_ref[here] = out_ref[here] + pass_buf[1, z, here].astype(f32)
+
+    for target in range(line):
+        for j in range(1, group):
+            across(j, target).wait_send()
+        for c in range(pieces):
+
+            @pl.when(target > z)
+            def _():
+                along(0, target, c).wait_send()
+
+            @pl.when(target < z)
+            def _():
+                along(1, target, c).wait_send()
 
 
 def scatter_plane(partial):
-    return lax.psum_scatter(partial, PLANE, scatter_dimension=0, tiled=True)
+    line, group = lax.axis_size("gz"), lax.axis_size("gy")
+    held = partial.shape[0] // (line * group)
+    block = partial.shape[1:]
+    others = max(group - 1, 1)
+    pieces = pieces_of(held)
+    return pl.pallas_call(
+        functools.partial(scatter_kernel, line, group),
+        out_shape=jax.ShapeDtypeStruct((held,) + block, jnp.float32),
+        in_specs=[VMEM],
+        out_specs=VMEM,
+        scratch_shapes=[
+            pltpu.VMEM((others, line, held) + block, partial.dtype),
+            pltpu.VMEM((line, held) + block, partial.dtype),
+            pltpu.VMEM((2, line, held) + block, partial.dtype),
+            pltpu.SemaphoreType.DMA((others, line)),
+            pltpu.SemaphoreType.DMA((others, line)),
+            pltpu.SemaphoreType.DMA((2, line, pieces)),
+            pltpu.SemaphoreType.DMA((2, line, pieces)),
+        ],
+        compiler_params=pltpu.CompilerParams(
+            collective_id=2, has_side_effects=True, vmem_limit_bytes=VMEM_LIMIT
+        ),
+    )(partial)
 
 
 def shards(
@@ -237,14 +557,16 @@
     slots = reads.shape[1]
     pairs = pairs_of(tables)
 
-    gathered = gather_plane(ham_blocks)
     sent_numbers = plane * lanes_count
-    numbers = jnp.concatenate([send_table.reshape(1, -1), table_pick.reshape(1, -1)], axis=1)
-    numbers = lax.all_gather(numbers, EVERY, axis=0, tiled=True)
+    own_picks = table_pick.reshape(1, -1)
+    numbers = jnp.concatenate([send_table.reshape(1, -1), own_picks], axis=1)
+    length = numbers.shape[1]
+    room = -(-length // 1024) * 1024
+    numbers = jnp.pad(numbers, ((0, 0), (0, room - length))).reshape(-1, 128)
+    gathered, numbers = gather_plane(ham_blocks, numbers)
+    numbers = numbers.reshape(plane, room)
     mine = lax.axis_index(PLANE)
-    owners = lax.axis_index("gx") * plane + jnp.arange(plane)
-    theirs = jnp.take(numbers, owners, axis=0)[:, :sent_numbers]
-    theirs = jnp.take(theirs.reshape(plane, plane, lanes_count), mine, axis=1)
+    theirs = lax.dynamic_slice(numbers, (0, mine * lanes_count), (plane, lanes_count))
     chosen = jnp.take(theirs.reshape(-1), entry_slot[0])
     bins = ((entry_slot[0] // lanes_count) * held + chosen).astype(jnp.int32)
 
@@ -285,8 +607,9 @@
     )(phi[0], potential.reshape(points // 128, 128))
     gathered_grams = face_stack(grams)
 
-    near = jnp.take(numbers, neighbour_numbers(), axis=0)[:, sent_numbers:]
-    near = near.reshape(7, 2, slots)
+    before, after = both_sides(own_picks, own_picks, "gx")
+    around = jnp.take(numbers[:, sent_numbers:length], neighbour_numbers(), axis=0)
+    near = jnp.concatenate([own_picks, before, after, around]).reshape(7, 2, slots)
     low = jnp.minimum(near[:, 0], near[:, 1])
     high = jnp.maximum(near[:, 0], near[:, 1])
     pair = low * tables - low * (low + 1) // 2 + high - low - 1
@@ -302,7 +625,7 @@
         flops=7 * slots * width * width,
         moved=plane * held * width * width * 2,
     )(place, column, flip, gathered_grams)
-    grid_blocks = scatter_plane(partial).astype(jnp.float32)
+    grid_blocks = scatter_plane(partial)
     return (potential, grid_blocks)
 
 

time: 215 us -> 141 us (0.66)
  blocking collectives: 68.2 us -> 0 us
  Pallas kernels: 17.8 us -> 77 us
  waiting for transfers between devices: 74 us -> 22.2 us
  between operations: 14.4 us -> 1.01 us
  starting transfers between devices: 23.8 us -> 26.1 us
    all_gather x1 -> x0, blocking collectives: 68.2 us -> none  [shards(): numbers = lax.all_gather(numbers, EVERY, axis=0, tiled=True)]
    pallas_call x0 -> x2, Pallas kernels: none -> 60.9 us  [the longest x1 36.9 us: scatter_plane(): pl.pallas_call(functools.partial(scatter_kernel, line, group), out_shape=...]
    reduce_scatter x1 -> x0, waiting for transfers between devices: 46.4 us -> none  [scatter_plane(): return lax.psum_scatter(partial, PLANE, scatter_dimension=0, tiled=True)]
    ppermute x12 -> x13, waiting for transfers between devices: 20.7 us -> 12.7 us  [both_sides(): below = lax.ppermute(high_part, axis, up)]
    ppermute x10 -> x11, waiting for transfers between devices: 6.76 us -> 9.51 us  [both_sides(): return (below, lax.ppermute(low_part, axis, down))]
    ppermute x10 -> x11, starting transfers between devices: 16.7 us -> 18.2 us  [both_sides(): return (below, lax.ppermute(low_part, axis, down))]
    ppermute x12 -> x13, starting transfers between devices: 6.95 us -> 7.88 us  [both_sides(): below = lax.ppermute(high_part, axis, up)]
    unnamed x29 -> x30, local copies, waits for them, and re-layouts: 4.86 us -> 5.69 us
  transfers between devices with their start and end apart: 24 -> 24, of which waited for: 15 -> 11; matrix products, arithmetic and copies ran while one was open for 4% -> 4% of each run, Pallas kernels for 4% -> 3%
where the time goes in v2:
time: 141 us
  Pallas kernels  77 us (55%)
  starting transfers between devices  26.1 us (19%)
  waiting for transfers between devices  22.2 us (16%)
  local copies, waits for them, and re-layouts  10.6 us (8%)
  other arithmetic  4.01 us (3%)
    pallas_call x1, Pallas kernels, scatter_plane(): pl.pallas_call(functools.partial(scatter_kernel, line, group), out_shape=...  36.9 us
    pallas_call x1, Pallas kernels, gather_plane(): pl.pallas_call(functools.partial(gather_kernel, line, group), out_shape=(...  24 us
    ppermute x11, starting transfers between devices, both_sides(): return (below, lax.ppermute(low_part, axis, down))  18.2 us
    ppermute x13, waiting for transfers between devices, both_sides(): below = lax.ppermute(high_part, axis, up)  12.7 us
    ppermute x11, waiting for transfers between devices, both_sides(): return (below, lax.ppermute(low_part, axis, down))  9.51 us
    ppermute x13, starting transfers between devices, both_sides(): below = lax.ppermute(high_part, axis, up)  7.88 us
    unnamed x30, local copies, waits for them, and re-layouts  5.69 us
    pallas_call x1, Pallas kernels, shards(): local_call(functools.partial(density_kernel, side), jax.ShapeDtypeStruct(...  4.45 us
  transfers between devices with their start and end apart: 24, of which 11 were waited for; matrix products, arithmetic and copies ran while one was open for 4% of the time, Pallas kernels for 3%

profile of v2, /device:TPU:0, one launch (start us, length us, event | category | flops | bytes accessed | tf_op | source)
XLA Modules:
  0.0 140.8 jit_solution(7961410320282514360)
XLA Ops:
  0.6 0.8 reshape.309
  1.4 0.8 copy.14
  2.3 1.0 copy-done
  3.3 24.0 %shard_map.104 = (bf16[64,128,128]{2,1,0:T(8,128)(2,1)S(1)}, s32[64,128]{1,0:T(8,128)S(1)}) custom-call(bf16[8,128,128]{2,1,0:T(8,128)(2,1)S(1)} %copy-done, s32[8,128]{1,0:T(8,128)S(1)} %bitcast.66), custom_call_target="tpu_custom_call" | custom-call | tf_op jit(solution)/shard_map/pallas_call | solution.py:371
  27.4 0.7 fusion.15
  28.1 0.8 gather_fusion
  28.9 0.7 fusion.14.bins_ref
  29.6 0.7 copy-done.4
  30.3 4.4 %shard_map.105 = bf16[6,128,128]{2,1,0:T(8,128)(2,1)S(1)} custom-call(s32[36]{0:T(128)S(1)} %fusion.14.bins_ref, bf16[64,128,128]{2,1,0:T(8,128)(2,1)S(1)} %get-tuple-element.5.blocks_ref, f32[1,768]{1,0:T(1,128)S(1)} %copy-done.4), custom_call_target="tpu_custom_call" | custom-call | flops 1811939328 | bytes 2097152 | tf_op jit(solution)/shard_map/pallas_call | solution.py:573
  34.7 1.6 %collective-permute-start = (bf16[6,128,128]{2,1,0:T(8,128)(2,1)S(1)}, bf16[6,128,128]{2,1,0:T(8,128)(2,1)S(1)}, u32[]{:S(2)}, u32[]{:S(2)}) collective-permute-start(bf16[6,128,128]{2,1,0:T(8,128)(2,1)S(1)} %shard_map.105), channel_id=1, source_target_pairs={{0,8},{8,16},{16,24},{24,0},{1,9},{9,17},{17,25},{25,1},{2,10},{10... | collective-permute-start | bytes 589832 | tf_op jit(solution)/shard_map/ppermute | solution.py:171
  36.3 1.4 %collective-permute-start.1 = (bf16[6,128,128]{2,1,0:T(8,128)(2,1)S(1)}, bf16[6,128,128]{2,1,0:T(8,128)(2,1)S(1)}, u32[]{:S(2)}, u32[]{:S(2)}) collective-permute-start(bf16[6,128,128]{2,1,0:T(8,128)(2,1)S(1)} %shard_map.105), channel_id=1, source_target_pairs={{8,0},{16,8},{24,16},{0,24},{9,1},{17,9},{25,17},{1,25},{10,2},{18... | collective-permute-start | bytes 589832 | tf_op jit(solution)/shard_map/ppermute | solution.py:174
  37.7 1.5 %collective-permute-start.18 = (s32[1,16]{1,0:T(1,128)S(1)}, s32[1,16]{1,0:T(1,128)S(1)}, u32[]{:S(2)}, u32[]{:S(2)}) collective-permute-start(s32[1,16]{1,0:T(1,128)S(1)} %reshape.309), channel_id=1, source_target_pairs={{8,0},{16,8},{24,16},{0,24},{9,1},{17,9},{25,17},{1,25},{10,2},{18... | collective-permute-start | bytes 200 | tf_op jit(solution)/shard_map/ppermute | solution.py:174
  39.9 0.6 gather_fusion.2
  40.6 0.8 gather_fusion.1
  41.7 5.5 %collective-permute-done.18 = s32[1,16]{1,0:T(1,128)S(1)} collective-permute-done((s32[1,16]{1,0:T(1,128)S(1)}, s32[1,16]{1,0:T(1,128)S(1)}, u32[]{:S(2)}, u32[]{:S(2)}) %collective-permute-start.18) | collective-permute-done | bytes 96 | tf_op jit(solution)/shard_map/ppermute | solution.py:174
  47.2 1.5 %collective-permute-start.17 = (s32[1,16]{1,0:T(1,128)S(1)}, s32[1,16]{1,0:T(1,128)S(1)}, u32[]{:S(2)}, u32[]{:S(2)}) collective-permute-start(s32[1,16]{1,0:T(1,128)S(1)} %reshape.309), channel_id=1, source_target_pairs={{0,8},{8,16},{16,24},{24,0},{1,9},{9,17},{17,25},{25,1},{2,10},{10... | collective-permute-start | bytes 200 | tf_op jit(solution)/shard_map/ppermute | solution.py:171
  48.7 0.5 broadcast.171
  49.2 0.7 reduce.14
  49.9 1.7 %collective-permute-done.17 = s32[1,16]{1,0:T(1,128)S(1)} collective-permute-done((s32[1,16]{1,0:T(1,128)S(1)}, s32[1,16]{1,0:T(1,128)S(1)}, u32[]{:S(2)}, u32[]{:S(2)}) %collective-permute-start.17) | collective-permute-done | bytes 96 | tf_op jit(solution)/shard_map/ppermute | solution.py:171
  51.6 2.5 %collective-permute-start.4 = (bf16[6,128,128]{2,1,0:T(8,128)(2,1)S(1)}, bf16[6,128,128]{2,1,0:T(8,128)(2,1)S(1)}, u32[]{:S(2)}, u32[]{:S(2)}) collective-permute-start(bf16[6,128,128]{2,1,0:T(8,128)(2,1)S(1)} %shard_map.105), channel_id=1, source_target_pairs={{1,0},{2,1},{3,2},{0,3},{5,4},{6,5},{7,6},{4,7},{9,8},{10,9},{11,1... | collective-permute-start | bytes 589832 | tf_op jit(solution)/shard_map/ppermute | solution.py:174
  54.1 0.7 reduce.15
  55.2 0.6 collective-permute-start.5
  55.9 2.4 %collective-permute-start.6 = (f32[1,8,128]{2,1,0:T(8,128)S(1)}, f32[1,8,128]{2,1,0:T(8,128)S(1)}, u32[]{:S(2)}, u32[]{:S(2)}) collective-permute-start(f32[1,8,128]{2,1,0:T(8,128)S(1)} %get-tuple-element.33), channel_id=1, source_target_pairs={{8,0},{16,8},{24,16},{0,24},{9,1},{17,9},{25,17},{1,25},{10,2},{18... | collective-permute-start | bytes 12296 | tf_op jit(solution)/shard_map/ppermute | solution.py:174
  58.5 0.6 collective-permute-start.8
  59.2 5.6 %collective-permute-done.9 = f32[4,8,1]{2,1,0:T(8,128)S(1)} collective-permute-done((f32[4,8,1]{2,1,0:T(8,128)S(1)}, f32[4,8,1]{2,1,0:T(8,128)S(1)}, u32[]{:S(2)}, u32[]{:S(2)}) %collective-permute-start.9) | collective-permute-done | bytes 160 | tf_op jit(solution)/shard_map/ppermute | solution.py:171
  64.8 0.6 collective-permute-start.10
  65.4 2.2 %copy-done.2 = bf16[1,4,128,4096]{3,2,1,0:T(8,128)(2,1)S(1)} copy-done((bf16[1,4,128,4096]{3,2,1,0:T(8,128)(2,1)S(1)}, bf16[1,4,128,4096]{3,2,1,0:T(8,128)(2,1)}, u32[]{:S(2)}) %copy-start.2) | copy-done | bytes 4194328
  67.5 4.4 %shard_map.106 = f32[32,128]{1,0:T(8,128)S(1)} custom-call(s32[8]{0:T(128)S(1)} %bitcast.70, s32[2,8]{1,0:T(2,128)S(1)} %bitcast.67, bf16[42,128,128]{2,1,0:T(8,128)(2,1)S(1)} %constant_dynamic-update-slice_fusion.blocks_ref, bf16[4,128,4096]{2,1,0:T(8,128)(2,1)S(1)} %bitcast.68), custom_call_target="tpu_custom_call" | custom-call | flops 2147483648 | bytes 4194304 | tf_op jit(solution)/shard_map/pallas_call | solution.py:587
  72.2 1.5 %collective-permute-start.15 = (f32[4,8,1]{2,1,0:T(8,128)S(1)}, f32[4,8,1]{2,1,0:T(8,128)S(1)}, u32[]{:S(2)}, u32[]{:S(2)}) collective-permute-start(f32[4,8,1]{2,1,0:T(8,128)S(1)} %get-tuple-element.22), channel_id=1, source_target_pairs={{0,1},{1,2},{2,3},{3,0},{4,5},{5,6},{6,7},{7,4},{8,9},{9,10},{10,1... | collective-permute-start | bytes 392 | tf_op jit(solution)/shard_map/ppermute | solution.py:171
  73.7 2.4 %collective-permute-start.16 = (f32[4,8,1]{2,1,0:T(8,128)S(1)}, f32[4,8,1]{2,1,0:T(8,128)S(1)}, u32[]{:S(2)}, u32[]{:S(2)}) collective-permute-start(f32[4,8,1]{2,1,0:T(8,128)S(1)} %get-tuple-element.21), channel_id=1, source_target_pairs={{1,0},{2,1},{3,2},{0,3},{5,4},{6,5},{7,6},{4,7},{9,8},{10,9},{11,1... | collective-permute-start | bytes 392 | tf_op jit(solution)/shard_map/ppermute | solution.py:174
  76.1 0.6 collective-permute-start.12
  76.7 1.5 %collective-permute-start.11 = (f32[1,8,128]{2,1,0:T(8,128)S(1)}, f32[1,8,128]{2,1,0:T(8,128)S(1)}, u32[]{:S(2)}, u32[]{:S(2)}) collective-permute-start(f32[1,8,128]{2,1,0:T(8,128)S(1)} %get-tuple-element.17), channel_id=1, source_target_pairs={{0,8},{8,16},{16,24},{24,0},{1,9},{9,17},{17,25},{25,1},{2,10},{10... | collective-permute-start | bytes 12296 | tf_op jit(solution)/shard_map/ppermute | solution.py:171
  78.2 0.5 collective-permute-start.13
  78.7 0.6 collective-permute-done.14
  79.5 0.2 collective-permute-done.12
  79.7 1.5 %collective-permute-done.11 = f32[1,8,128]{2,1,0:T(8,128)S(1)} collective-permute-done((f32[1,8,128]{2,1,0:T(8,128)S(1)}, f32[1,8,128]{2,1,0:T(8,128)S(1)}, u32[]{:S(2)}, u32[]{:S(2)}) %collective-permute-start.11) | collective-permute-done | bytes 4128 | tf_op jit(solution)/shard_map/ppermute | solution.py:171
  81.3 3.2 %shard_map.107 = bf16[6,128,128]{2,1,0:T(8,128)(2,1)S(1)} custom-call(bf16[4,128,4096]{2,1,0:T(8,128)(2,1)S(1)} %bitcast.69, f32[32,128]{1,0:T(8,128)S(1)} %fusion.9.v_ref), custom_call_target="tpu_custom_call" | custom-call | flops 2147483648 | bytes 4194304 | tf_op jit(solution)/shard_map/pallas_call | solution.py:600
  84.5 0.6 collective-permute-start.19
  85.1 2.4 %collective-permute-start.20 = (bf16[6,128,128]{2,1,0:T(8,128)(2,1)S(1)}, bf16[6,128,128]{2,1,0:T(8,128)(2,1)S(1)}, u32[]{:S(2)}, u32[]{:S(2)}) collective-permute-start(bf16[6,128,128]{2,1,0:T(8,128)(2,1)S(1)} %shard_map.107), channel_id=1, source_target_pairs={{8,0},{16,8},{24,16},{0,24},{9,1},{17,9},{25,17},{1,25},{10,2},{18... | collective-permute-start | bytes 589832 | tf_op jit(solution)/shard_map/ppermute | solution.py:174
  87.5 3.8 %collective-permute-start.23 = (bf16[6,128,128]{2,1,0:T(8,128)(2,1)S(1)}, bf16[6,128,128]{2,1,0:T(8,128)(2,1)S(1)}, u32[]{:S(2)}, u32[]{:S(2)}) collective-permute-start(bf16[6,128,128]{2,1,0:T(8,128)(2,1)S(1)} %shard_map.107), channel_id=1, source_target_pairs={{1,0},{2,1},{3,2},{0,3},{5,4},{6,5},{7,6},{4,7},{9,8},{10,9},{11,1... | collective-permute-start | bytes 589832 | tf_op jit(solution)/shard_map/ppermute | solution.py:174
  91.3 0.7 fusion.7
  92.0 1.0 collective-permute-done.19
  93.1 1.1 collective-permute-done.20
  94.3 2.7 %collective-permute-done.22 = bf16[6,128,128]{2,1,0:T(8,128)(2,1)S(1)} collective-permute-done((bf16[6,128,128]{2,1,0:T(8,128)(2,1)S(1)}, bf16[6,128,128]{2,1,0:T(8,128)(2,1)S(1)}, u32[]{:S(2)}, u32[]{:S(2)}) %collective-permute-start.22) | collective-permute-done | bytes 196640 | tf_op jit(solution)/shard_map/ppermute | solution.py:171
  97.1 2.0 %collective-permute-done.23 = bf16[6,128,128]{2,1,0:T(8,128)(2,1)S(1)} collective-permute-done((bf16[6,128,128]{2,1,0:T(8,128)(2,1)S(1)}, bf16[6,128,128]{2,1,0:T(8,128)(2,1)S(1)}, u32[]{:S(2)}, u32[]{:S(2)}) %collective-permute-start.23) | collective-permute-done | bytes 196640 | tf_op jit(solution)/shard_map/ppermute | solution.py:174
  99.1 4.1 %shard_map.108.x_ref = bf16[64,128,128]{2,1,0:T(8,128)(2,1)S(1)} custom-call(s32[56]{0:T(128)S(1)} %and_select_fusion.1.bin_ref, s32[56]{0:T(128)S(1)} %add_add_fusion.col_ref, s32[56]{0:T(128)S(1)} %reshape.314.flip_ref, bf16[42,128,128]{2,1,0:T(8,128)(2,1)S(1)} %constant_dynamic-update-slice_fusion.7.blocks_ref), custom_call_target="tpu_custom_call" | custom-call | flops 917504 | bytes 2097152 | tf_op jit(solution)/shard_map/pallas_call | solution.py:620
  103.1 36.9 %shard_map.109 = f32[8,128,128]{2,1,0:T(8,128)S(1)} custom-call(bf16[64,128,128]{2,1,0:T(8,128)(2,1)S(1)} %shard_map.108.x_ref), custom_call_target="tpu_custom_call" | custom-call | tf_op jit(solution)/shard_map/pallas_call | solution.py:527
  140.1 0.8 copy.30
  (92 shorter events, 2.9 us)
Async XLA Ops:
  2.3 1.0 copy-start
  29.6 0.7 copy-start.4
  30.2 9.0 %copy-start.6 = (f32[4,8,128]{2,1,0:T(8,128)S(1)}, f32[4,8,128]{2,1,0:T(8,128)}, u32[]{:S(2)}) copy-start(f32[4,8,128]{2,1,0:T(8,128)} %param.17) | copy-start | bytes 49156
  30.2 9.2 %copy-start.7 = (s32[1,7,8]{2,0,1:T(1,128)S(1)}, s32[1,7,8]{2,0,1:T(1,128)}, u32[]{:S(2)}) copy-start(s32[1,7,8]{2,0,1:T(1,128)} %param.14) | copy-start | bytes 676
  34.7 20.2 %copy-start.1 = (s32[1,2,8]{2,1,0:T(2,128)S(1)}, s32[1,2,8]{2,1,0:T(2,128)}, u32[]{:S(2)}) copy-start(s32[1,2,8]{2,1,0:T(2,128)} %param.15) | copy-start | bytes 196
  34.7 20.5 %collective-permute-start = (bf16[6,128,128]{2,1,0:T(8,128)(2,1)S(1)}, bf16[6,128,128]{2,1,0:T(8,128)(2,1)S(1)}, u32[]{:S(2)}, u32[]{:S(2)}) collective-permute-start(bf16[6,128,128]{2,1,0:T(8,128)(2,1)S(1)} %shard_map.105), channel_id=1, source_target_pairs={{0,8},{8,16},{16,24},{24,0},{1,9},{9,17},{17,25},{25,1},{2,10},{10... | collective-permute-start | bytes 589832 | tf_op jit(solution)/shard_map/ppermute | solution.py:171
  36.3 19.6 %collective-permute-start.1 = (bf16[6,128,128]{2,1,0:T(8,128)(2,1)S(1)}, bf16[6,128,128]{2,1,0:T(8,128)(2,1)S(1)}, u32[]{:S(2)}, u32[]{:S(2)}) collective-permute-start(bf16[6,128,128]{2,1,0:T(8,128)(2,1)S(1)} %shard_map.105), channel_id=1, source_target_pairs={{8,0},{16,8},{24,16},{0,24},{9,1},{17,9},{25,17},{1,25},{10,2},{18... | collective-permute-start | bytes 589832 | tf_op jit(solution)/shard_map/ppermute | solution.py:174
  37.7 20.6 %collective-permute-start.2 = (bf16[6,128,128]{2,1,0:T(8,128)(2,1)S(1)}, bf16[6,128,128]{2,1,0:T(8,128)(2,1)S(1)}, u32[]{:S(2)}, u32[]{:S(2)}) collective-permute-start(bf16[6,128,128]{2,1,0:T(8,128)(2,1)S(1)} %shard_map.105), channel_id=1, source_target_pairs={{0,4},{4,0},{1,5},{5,1},{2,6},{6,2},{3,7},{7,3},{8,12},{12,8},{9,1... | collective-permute-start | bytes 589832 | tf_op jit(solution)/shard_map/ppermute | solution.py:171
  37.7 20.7 %collective-permute-start.3 = (bf16[6,128,128]{2,1,0:T(8,128)(2,1)S(1)}, bf16[6,128,128]{2,1,0:T(8,128)(2,1)S(1)}, u32[]{:S(2)}, u32[]{:S(2)}) collective-permute-start(bf16[6,128,128]{2,1,0:T(8,128)(2,1)S(1)} %shard_map.105), channel_id=1, source_target_pairs={{0,1},{1,2},{2,3},{3,0},{4,5},{5,6},{6,7},{7,4},{8,9},{9,10},{10,1... | collective-permute-start | bytes 589832 | tf_op jit(solution)/shard_map/ppermute | solution.py:171
  37.7 9.5 %collective-permute-start.18 = (s32[1,16]{1,0:T(1,128)S(1)}, s32[1,16]{1,0:T(1,128)S(1)}, u32[]{:S(2)}, u32[]{:S(2)}) collective-permute-start(s32[1,16]{1,0:T(1,128)S(1)} %reshape.309), channel_id=1, source_target_pairs={{8,0},{16,8},{24,16},{0,24},{9,1},{17,9},{25,17},{1,25},{10,2},{18... | collective-permute-start | bytes 200 | tf_op jit(solution)/shard_map/ppermute | solution.py:174
  40.6 24.8 %copy-start.5 = (s32[1,8]{1,0:T(1,128)S(1)}, s32[1,8]{1,0:T(1,128)}, u32[]{:S(2)}) copy-start(s32[1,8]{1,0:T(1,128)} %param.13) | copy-start | bytes 100
  47.2 4.4 %collective-permute-start.17 = (s32[1,16]{1,0:T(1,128)S(1)}, s32[1,16]{1,0:T(1,128)S(1)}, u32[]{:S(2)}, u32[]{:S(2)}) collective-permute-start(s32[1,16]{1,0:T(1,128)S(1)} %reshape.309), channel_id=1, source_target_pairs={{0,8},{8,16},{16,24},{24,0},{1,9},{9,17},{17,25},{25,1},{2,10},{10... | collective-permute-start | bytes 200 | tf_op jit(solution)/shard_map/ppermute | solution.py:171
  51.6 7.4 %collective-permute-start.4 = (bf16[6,128,128]{2,1,0:T(8,128)(2,1)S(1)}, bf16[6,128,128]{2,1,0:T(8,128)(2,1)S(1)}, u32[]{:S(2)}, u32[]{:S(2)}) collective-permute-start(bf16[6,128,128]{2,1,0:T(8,128)(2,1)S(1)} %shard_map.105), channel_id=1, source_target_pairs={{1,0},{2,1},{3,2},{0,3},{5,4},{6,5},{7,6},{4,7},{9,8},{10,9},{11,1... | collective-permute-start | bytes 589832 | tf_op jit(solution)/shard_map/ppermute | solution.py:174
  55.2 16.8 %collective-permute-start.5 = (f32[1,8,128]{2,1,0:T(8,128)S(1)}, f32[1,8,128]{2,1,0:T(8,128)S(1)}, u32[]{:S(2)}, u32[]{:S(2)}) collective-permute-start(f32[1,8,128]{2,1,0:T(8,128)S(1)} %get-tuple-element.34), channel_id=1, source_target_pairs={{0,8},{8,16},{16,24},{24,0},{1,9},{9,17},{17,25},{25,1},{2,10},{10... | collective-permute-start | bytes 12296 | tf_op jit(solution)/shard_map/ppermute | solution.py:171
  55.9 16.1 %collective-permute-start.6 = (f32[1,8,128]{2,1,0:T(8,128)S(1)}, f32[1,8,128]{2,1,0:T(8,128)S(1)}, u32[]{:S(2)}, u32[]{:S(2)}) collective-permute-start(f32[1,8,128]{2,1,0:T(8,128)S(1)} %get-tuple-element.33), channel_id=1, source_target_pairs={{8,0},{16,8},{24,16},{0,24},{9,1},{17,9},{25,17},{1,25},{10,2},{18... | collective-permute-start | bytes 12296 | tf_op jit(solution)/shard_map/ppermute | solution.py:174
  58.3 13.6 %collective-permute-start.7 = (f32[4,1,128]{2,1,0:T(1,128)S(1)}, f32[4,1,128]{2,1,0:T(1,128)S(1)}, u32[]{:S(2)}, u32[]{:S(2)}) collective-permute-start(f32[4,1,128]{2,1,0:T(1,128)S(1)} %get-tuple-element.30), channel_id=1, source_target_pairs={{0,4},{4,0},{1,5},{5,1},{2,6},{6,2},{3,7},{7,3},{8,12},{12,8},{9,1... | collective-permute-start | bytes 6152 | tf_op jit(solution)/shard_map/ppermute | solution.py:171
  58.5 13.5 %collective-permute-start.8 = (f32[4,1,128]{2,1,0:T(1,128)S(1)}, f32[4,1,128]{2,1,0:T(1,128)S(1)}, u32[]{:S(2)}, u32[]{:S(2)}) collective-permute-start(f32[4,1,128]{2,1,0:T(1,128)S(1)} %get-tuple-element.29), channel_id=1, source_target_pairs={{4,0},{0,4},{5,1},{1,5},{6,2},{2,6},{7,3},{3,7},{12,8},{8,12},{13,... | collective-permute-start | bytes 6152 | tf_op jit(solution)/shard_map/ppermute | solution.py:174
  59.1 5.7 %collective-permute-start.9 = (f32[4,8,1]{2,1,0:T(8,128)S(1)}, f32[4,8,1]{2,1,0:T(8,128)S(1)}, u32[]{:S(2)}, u32[]{:S(2)}) collective-permute-start(f32[4,8,1]{2,1,0:T(8,128)S(1)} %get-tuple-element.26), channel_id=1, source_target_pairs={{0,1},{1,2},{2,3},{3,0},{4,5},{5,6},{6,7},{7,4},{8,9},{9,10},{10,1... | collective-permute-start | bytes 392 | tf_op jit(solution)/shard_map/ppermute | solution.py:171
  64.8 7.2 %collective-permute-start.10 = (f32[4,8,1]{2,1,0:T(8,128)S(1)}, f32[4,8,1]{2,1,0:T(8,128)S(1)}, u32[]{:S(2)}, u32[]{:S(2)}) collective-permute-start(f32[4,8,1]{2,1,0:T(8,128)S(1)} %get-tuple-element.25), channel_id=1, source_target_pairs={{1,0},{2,1},{3,2},{0,3},{5,4},{6,5},{7,6},{4,7},{9,8},{10,9},{11,1... | collective-permute-start | bytes 392 | tf_op jit(solution)/shard_map/ppermute | solution.py:174
  65.4 2.2 %copy-start.2 = (bf16[1,4,128,4096]{3,2,1,0:T(8,128)(2,1)S(1)}, bf16[1,4,128,4096]{3,2,1,0:T(8,128)(2,1)}, u32[]{:S(2)}) copy-start(bf16[1,4,128,4096]{3,2,1,0:T(8,128)(2,1)} %param.16) | copy-start | bytes 12582916
  67.5 13.7 %copy-start.3 = (bf16[1,4,128,4096]{3,2,1,0:T(8,128)(2,1)S(1)}, bf16[1,4,128,4096]{3,2,1,0:T(8,128)(2,1)}, u32[]{:S(2)}) copy-start(bf16[1,4,128,4096]{3,2,1,0:T(8,128)(2,1)} %param.16) | copy-start | bytes 12582916
  72.2 5.9 %collective-permute-start.15 = (f32[4,8,1]{2,1,0:T(8,128)S(1)}, f32[4,8,1]{2,1,0:T(8,128)S(1)}, u32[]{:S(2)}, u32[]{:S(2)}) collective-permute-start(f32[4,8,1]{2,1,0:T(8,128)S(1)} %get-tuple-element.22), channel_id=1, source_target_pairs={{0,1},{1,2},{2,3},{3,0},{4,5},{5,6},{6,7},{7,4},{8,9},{9,10},{10,1... | collective-permute-start | bytes 392 | tf_op jit(solution)/shard_map/ppermute | solution.py:171
  73.7 4.9 %collective-permute-start.16 = (f32[4,8,1]{2,1,0:T(8,128)S(1)}, f32[4,8,1]{2,1,0:T(8,128)S(1)}, u32[]{:S(2)}, u32[]{:S(2)}) collective-permute-start(f32[4,8,1]{2,1,0:T(8,128)S(1)} %get-tuple-element.21), channel_id=1, source_target_pairs={{1,0},{2,1},{3,2},{0,3},{5,4},{6,5},{7,6},{4,7},{9,8},{10,9},{11,1... | collective-permute-start | bytes 392 | tf_op jit(solution)/shard_map/ppermute | solution.py:174
  76.1 3.6 %collective-permute-start.12 = (f32[1,8,128]{2,1,0:T(8,128)S(1)}, f32[1,8,128]{2,1,0:T(8,128)S(1)}, u32[]{:S(2)}, u32[]{:S(2)}) collective-permute-start(f32[1,8,128]{2,1,0:T(8,128)S(1)} %get-tuple-element.18), channel_id=1, source_target_pairs={{8,0},{16,8},{24,16},{0,24},{9,1},{17,9},{25,17},{1,25},{10,2},{18... | collective-permute-start | bytes 12296 | tf_op jit(solution)/shard_map/ppermute | solution.py:174
  76.7 4.5 %collective-permute-start.11 = (f32[1,8,128]{2,1,0:T(8,128)S(1)}, f32[1,8,128]{2,1,0:T(8,128)S(1)}, u32[]{:S(2)}, u32[]{:S(2)}) collective-permute-start(f32[1,8,128]{2,1,0:T(8,128)S(1)} %get-tuple-element.17), channel_id=1, source_target_pairs={{0,8},{8,16},{16,24},{24,0},{1,9},{9,17},{17,25},{25,1},{2,10},{10... | collective-permute-start | bytes 12296 | tf_op jit(solution)/shard_map/ppermute | solution.py:171
  78.1 1.2 collective-permute-start.14
  78.2 1.3 collective-permute-start.13
  84.5 8.5 %collective-permute-start.19 = (bf16[6,128,128]{2,1,0:T(8,128)(2,1)S(1)}, bf16[6,128,128]{2,1,0:T(8,128)(2,1)S(1)}, u32[]{:S(2)}, u32[]{:S(2)}) collective-permute-start(bf16[6,128,128]{2,1,0:T(8,128)(2,1)S(1)} %shard_map.107), channel_id=1, source_target_pairs={{0,8},{8,16},{16,24},{24,0},{1,9},{9,17},{17,25},{25,1},{2,10},{10... | collective-permute-start | bytes 589832 | tf_op jit(solution)/shard_map/ppermute | solution.py:171
  85.1 9.1 %collective-permute-start.20 = (bf16[6,128,128]{2,1,0:T(8,128)(2,1)S(1)}, bf16[6,128,128]{2,1,0:T(8,128)(2,1)S(1)}, u32[]{:S(2)}, u32[]{:S(2)}) collective-permute-start(bf16[6,128,128]{2,1,0:T(8,128)(2,1)S(1)} %shard_map.107), channel_id=1, source_target_pairs={{8,0},{16,8},{24,16},{0,24},{9,1},{17,9},{25,17},{1,25},{10,2},{18... | collective-permute-start | bytes 589832 | tf_op jit(solution)/shard_map/ppermute | solution.py:174
  87.5 6.7 %collective-permute-start.21 = (bf16[6,128,128]{2,1,0:T(8,128)(2,1)S(1)}, bf16[6,128,128]{2,1,0:T(8,128)(2,1)S(1)}, u32[]{:S(2)}, u32[]{:S(2)}) collective-permute-start(bf16[6,128,128]{2,1,0:T(8,128)(2,1)S(1)} %shard_map.107), channel_id=1, source_target_pairs={{0,4},{4,0},{1,5},{5,1},{2,6},{6,2},{3,7},{7,3},{8,12},{12,8},{9,1... | collective-permute-start | bytes 589832 | tf_op jit(solution)/shard_map/ppermute | solution.py:171
  87.5 9.5 %collective-permute-start.22 = (bf16[6,128,128]{2,1,0:T(8,128)(2,1)S(1)}, bf16[6,128,128]{2,1,0:T(8,128)(2,1)S(1)}, u32[]{:S(2)}, u32[]{:S(2)}) collective-permute-start(bf16[6,128,128]{2,1,0:T(8,128)(2,1)S(1)} %shard_map.107), channel_id=1, source_target_pairs={{0,1},{1,2},{2,3},{3,0},{4,5},{5,6},{6,7},{7,4},{8,9},{9,10},{10,1... | collective-permute-start | bytes 589832 | tf_op jit(solution)/shard_map/ppermute | solution.py:171
  87.5 11.5 %collective-permute-start.23 = (bf16[6,128,128]{2,1,0:T(8,128)(2,1)S(1)}, bf16[6,128,128]{2,1,0:T(8,128)(2,1)S(1)}, u32[]{:S(2)}, u32[]{:S(2)}) collective-permute-start(bf16[6,128,128]{2,1,0:T(8,128)(2,1)S(1)} %shard_map.107), channel_id=1, source_target_pairs={{1,0},{2,1},{3,2},{0,3},{5,4},{6,5},{7,6},{4,7},{9,8},{10,9},{11,1... | collective-permute-start | bytes 589832 | tf_op jit(solution)/shard_map/ppermute | solution.py:174

commit v3 on v2

--- a/solution.py
+++ b/solution.py
@@ -16,14 +16,14 @@
 MESH = pl.DeviceIdType.MESH
 
 
-def local_call(kernel, out_shape, in_specs, scratch=(), flops=0, moved=0):
+def local_call(kernel, out_shape, in_specs, scratch=(), flops=0, moved=0, limit=24 * 1024 * 1024):
     return pl.pallas_call(
         kernel,
         out_shape=out_shape,
         in_specs=in_specs,
         out_specs=VMEM,
         scratch_shapes=scratch,
-        compiler_params=pltpu.CompilerParams(vmem_limit_bytes=VMEM_LIMIT),
+        compiler_params=pltpu.CompilerParams(vmem_limit_bytes=limit),
         cost_estimate=pl.CostEstimate(flops=flops, bytes_accessed=moved, transcendentals=0),
     )
 
@@ -162,40 +162,74 @@
     out_ref[...] = acc_ref[...].astype(jnp.bfloat16)
 
 
-def both_sides(low_part, high_part, axis):
-    count = lax.axis_size(axis)
-    if count == 1:
-        return high_part, low_part
-    up = [(i, (i + 1) % count) for i in range(count)]
-    down = [((i + 1) % count, i) for i in range(count)]
-    below = lax.ppermute(high_part, axis, up)
-    if count == 2 and low_part is high_part:
-        return below, below
-    return below, lax.ppermute(low_part, axis, down)
-
-
-def face_stack(block):
-    parts = [block]
-    for axis in EVERY:
-        parts.extend(both_sides(block, block, axis))
-    return jnp.concatenate(parts)
-
-
-def faces_of(field):
-    got = []
-    for dim, axis in enumerate(EVERY):
-        size = field.shape[dim]
-        low = lax.slice_in_dim(field, 0, 1, axis=dim)
-        high = lax.slice_in_dim(field, size - 1, size, axis=dim)
-        got.append(both_sides(low, high, axis))
-    return got
-
-
-def jacobi_step(field, faces, source):
+def face_kernel(counts, kinds, *refs):
+    ins, outs = refs[:kinds], refs[kinds : 2 * kinds]
+    send_sem, recv_sem = refs[2 * kinds :]
+    barrier = pltpu.get_barrier_semaphore()
+    copies = []
+    for n, (axis, count) in enumerate(zip(EVERY, counts)):
+        here = lax.axis_index(axis)
+        for face, step in ((2 * n + 1, 1), (2 * n + 2, count - 1)):
+            if count == 1 or (count == 2 and face % 2 == 0):
+                continue
+            copies.append((axis, lax.rem(here + step, count), face))
+    for axis, peer, _ in copies:
+        pl.semaphore_signal(barrier, inc=1, device_id={axis: peer}, device_id_type=MESH)
+    pl.semaphore_wait(barrier, len(copies))
+    started = []
+    for i in range(kinds):
+        for axis, peer, face in sorted(copies, key=lambda item: item[0] == "gy"):
+            copy = pltpu.make_async_remote_copy(
+                src_ref=ins[i],
+                dst_ref=outs[i].at[face],
+                send_sem=send_sem.at[i, face],
+                recv_sem=recv_sem.at[i, face],
+                device_id={axis: peer},
+                device_id_type=MESH,
+            )
+            copy.start()
+            started.append(copy)
+    for i in range(kinds):
+        outs[i][0] = ins[i][...]
+        for n, count in enumerate(counts):
+            if count == 1:
+                outs[i][2 * n + 1] = ins[i][...]
+                outs[i][2 * n + 2] = ins[i][...]
+    for copy in started:
+        copy.wait_recv()
+    for i in range(kinds):
+        for n, count in enumerate(counts):
+            if count == 2:
+                outs[i][2 * n + 2] = outs[i][2 * n + 1]
+    for copy in started:
+        copy.wait_send()
+
+
+def face_stack(number, *arrays):
+    counts = [lax.axis_size(axis) for axis in EVERY]
+    kinds = len(arrays)
+    return pl.pallas_call(
+        functools.partial(face_kernel, counts, kinds),
+        out_shape=tuple(jax.ShapeDtypeStruct((7,) + a.shape, a.dtype) for a in arrays),
+        in_specs=[VMEM] * kinds,
+        out_specs=(VMEM,) * kinds,
+        scratch_shapes=[
+            pltpu.SemaphoreType.DMA((kinds, 7)),
+            pltpu.SemaphoreType.DMA((kinds, 7)),
+        ],
+        compiler_params=pltpu.CompilerParams(
+            collective_id=number, has_side_effects=True, vmem_limit_bytes=12 * 1024 * 1024
+        ),
+    )(*arrays)
+
+
+def jacobi_step(fields, source):
+    field = fields[0]
     beside_all = source
     for dim in range(3):
-        below, above = faces[dim]
         size = field.shape[dim]
+        below = lax.slice_in_dim(fields[2 * dim + 1], size - 1, size, axis=dim)
+        above = lax.slice_in_dim(fields[2 * dim + 2], 0, 1, axis=dim)
         beside_all = beside_all + jnp.concatenate(
             [below, lax.slice_in_dim(field, 0, size - 1, axis=dim)], axis=dim
         )
@@ -203,15 +237,6 @@
             [lax.slice_in_dim(field, 1, size, axis=dim), above], axis=dim
         )
     return beside_all / 6.0
-
-
-def neighbour_numbers():
-    rows, line = lax.axis_size("gy"), lax.axis_size("gz")
-    row, z = lax.axis_index("gy"), lax.axis_index("gz")
-    places = []
-    for i, k in ((-1, 0), (1, 0), (0, -1), (0, 1)):
-        places.append((row + i + rows) % rows * line + (z + k + line) % line)
-    return jnp.stack(places)
 
 
 def greet_plane(line, group, z, row):
@@ -383,7 +408,7 @@
             pltpu.SemaphoreType.DMA((others, line, 2)),
         ],
         compiler_params=pltpu.CompilerParams(
-            collective_id=1, has_side_effects=True, vmem_limit_bytes=VMEM_LIMIT
+            collective_id=1, has_side_effects=True, vmem_limit_bytes=min(3 * blocks.nbytes * plane + 2**23, VMEM_LIMIT)
         ),
     )(blocks, numbers)
 
@@ -563,6 +588,7 @@
     length = numbers.shape[1]
     room = -(-length // 1024) * 1024
     numbers = jnp.pad(numbers, ((0, 0), (0, room - length))).reshape(-1, 128)
+    own_numbers = numbers
     gathered, numbers = gather_plane(ham_blocks, numbers)
     numbers = numbers.reshape(plane, room)
     mine = lax.axis_index(PLANE)
@@ -582,8 +608,8 @@
         flops=4 * order**3,
         moved=gathered.size * 2,
     )(bins, gathered, onsite)
-    candidates = face_stack(density)
-    first_faces = faces_of(potential_in)
+    candidates, fields, around = face_stack(3, density, potential_in, own_numbers)
+    candidates = candidates.reshape(7 * side, width, width)
     source = local_call(
         source_kernel,
         jax.ShapeDtypeStruct((points // 128, 128), jnp.float32),
@@ -595,8 +621,8 @@
         flops=2 * points * (tables * width) ** 2,
         moved=phi.size * 2,
     )(reads[0], table_pick[0], candidates, phi[0]).reshape(potential_in.shape)
-    potential = jacobi_step(potential_in, first_faces, source)
-    potential = jacobi_step(potential, faces_of(potential), source)
+    potential = jacobi_step(fields, source)
+    potential = jacobi_step(face_stack(4, potential)[0], source)
     grams = local_call(
         gram_kernel,
         jax.ShapeDtypeStruct((len(pairs), width, width), jnp.bfloat16),
@@ -605,11 +631,9 @@
         flops=2 * points * (tables * width) ** 2,
         moved=phi.size * 2,
     )(phi[0], potential.reshape(points // 128, 128))
-    gathered_grams = face_stack(grams)
-
-    before, after = both_sides(own_picks, own_picks, "gx")
-    around = jnp.take(numbers[:, sent_numbers:length], neighbour_numbers(), axis=0)
-    near = jnp.concatenate([own_picks, before, after, around]).reshape(7, 2, slots)
+    gathered_grams = face_stack(5, grams)[0].reshape(7 * len(pairs), width, width)
+
+    near = around.reshape(7, room)[:, sent_numbers:length].reshape(7, 2, slots)
     low = jnp.minimum(near[:, 0], near[:, 1])
     high = jnp.maximum(near[:, 0], near[:, 1])
     pair = low * tables - low * (low + 1) // 2 + high - low - 1
@@ -624,6 +648,7 @@
         [pltpu.VMEM((plane * held, width, width), jnp.float32)],
         flops=7 * slots * width * width,
         moved=plane * held * width * width * 2,
+        limit=min(7 * plane * held * width * width + 2**23, VMEM_LIMIT),
     )(place, column, flip, gathered_grams)
     grid_blocks = scatter_plane(partial)
     return (potential, grid_blocks)

time: 141 us -> 125 us (0.89)
  Pallas kernels: 77 us -> 109 us
  starting transfers between devices: 26.1 us -> 0 us
  waiting for transfers between devices: 22.2 us -> 0 us
    pallas_call x0 -> x3, Pallas kernels: none -> 32.1 us  [face_stack(): pl.pallas_call(functools.partial(face_kernel, counts, kinds), out_shape=t...]
    ppermute x24 -> x0, starting transfers between devices: 26.1 us -> none  [the longest x11 18.2 us: both_sides(): return (below, lax.ppermute(low_part, axis, down))]
    ppermute x24 -> x0, waiting for transfers between devices: 22.2 us -> none  [the longest x13 12.7 us: both_sides(): below = lax.ppermute(high_part, axis, up)]
    unnamed x30 -> x17, local copies, waits for them, and re-layouts: 5.69 us -> 7.58 us
  transfers between devices with their start and end apart: 24 -> 0, of which waited for: 11 -> 0; matrix products, arithmetic and copies ran while one was open for 4% -> 0% of each run, Pallas kernels for 3% -> 0%
where the time goes in v3:
time: 125 us; the launch traced here: 124 us
  Pallas kernels  109 us (87%)
  local copies, waits for them, and re-layouts  11.2 us (9%)
  other arithmetic  3.12 us (2%)
    pallas_call x1, Pallas kernels, scatter_plane(): pl.pallas_call(functools.partial(scatter_kernel, line, group), out_shape=...  36.2 us
    pallas_call x3, Pallas kernels, face_stack(): pl.pallas_call(functools.partial(face_kernel, counts, kinds), out_shape=t...  32.1 us
    pallas_call x1, Pallas kernels, gather_plane(): pl.pallas_call(functools.partial(gather_kernel, line, group), out_shape=(...  24 us
    unnamed x17, local copies, waits for them, and re-layouts  7.58 us
    pallas_call x1, Pallas kernels, shards(): local_call(functools.partial(density_kernel, side), jax.ShapeDtypeStruct(...  4.45 us
    pallas_call x1, Pallas kernels, shards(): local_call(combine_kernel, jax.ShapeDtypeStruct((plane * held, width, wid...  4.4 us
    pallas_call x1, Pallas kernels, shards(): local_call(source_kernel, jax.ShapeDtypeStruct((points // 128, 128), jnp....  4.38 us
    pallas_call x1, Pallas kernels, shards(): local_call(gram_kernel, jax.ShapeDtypeStruct((len(pairs), width, width),...  3.24 us

profile of v3, /device:TPU:0, one launch (start us, length us, event | category | flops | bytes accessed | tf_op | source)
XLA Modules:
  0.0 123.9 jit_solution(17178285251508454824)
XLA Ops:
  0.6 0.7 fusion.15
  1.3 0.8 reshape.137
  2.1 0.1 add.154
  2.1 0.1 add.155
  2.2 0.7 reduce
  2.9 0.1 reshape_squeeze.6
  3.0 0.1 reshape_squeeze.5
  3.1 0.8 copy.14
  3.9 0.1 reshape.136
  3.9 0.1 pad_add_fusion
  4.0 0.0 copy-start
  4.0 1.0 copy-done
  5.0 24.0 %shard_map.104 = (bf16[64,128,128]{2,1,0:T(8,128)(2,1)S(1)}, s32[64,128]{1,0:T(8,128)S(1)}) custom-call(bf16[8,128,128]{2,1,0:T(8,128)(2,1)S(1)} %copy-done, s32[8,128]{1,0:T(8,128)S(1)} %bitcast.102), custom_call_target="tpu_custom_call" | custom-call | tf_op jit(solution)/shard_map/pallas_call | solution.py:396
  29.0 0.1 constant_dynamic-slice_fusion
  29.1 0.1 reshape.140
  29.1 0.8 gather_fusion
  29.9 0.7 fusion.14.bins_ref
  30.6 0.0 copy-start.4
  30.6 0.7 copy-done.4
  31.3 4.4 %shard_map.105.refs_0_ = bf16[6,128,128]{2,1,0:T(8,128)(2,1)S(1)} custom-call(s32[36]{0:T(128)S(1)} %fusion.14.bins_ref, bf16[64,128,128]{2,1,0:T(8,128)(2,1)S(1)} %get-tuple-element.8.blocks_ref, f32[1,768]{1,0:T(1,128)S(1)} %copy-done.4), custom_call_target="tpu_custom_call" | custom-call | flops 1811939328 | bytes 2097152 | tf_op jit(solution)/shard_map/pallas_call | solution.py:599
  35.7 0.1 pad_add_fusion.1
  35.8 0.8 gather_fusion.1
  36.6 0.0 copy-done.1
  36.6 15.7 %shard_map.106 = (bf16[7,6,128,128]{3,2,1,0:T(8,128)(2,1)S(1)}, f32[7,4,8,128]{3,2,1,0:T(8,128)S(1)}, s32[7,8,128]{2,1,0:T(8,128)S(1)}) custom-call(bf16[6,128,128]{2,1,0:T(8,128)(2,1)S(1)} %shard_map.105.refs_0_, f32[4,8,128]{2,1,0:T(8,128)S(1)} %copy-done.1, s32[8,128]{1,0:T(8,128)S(1)} %bitcast.103), custom_call_target="tpu_custom_call" | custom-call | tf_op jit(solution)/shard_map/pallas_call | solution.py:211
  52.3 0.0 copy-done.5
  52.3 0.0 copy-done.6
  52.3 0.0 copy-start.2
  52.3 2.2 %copy-done.2 = bf16[1,4,128,4096]{3,2,1,0:T(8,128)(2,1)S(1)} copy-done((bf16[1,4,128,4096]{3,2,1,0:T(8,128)(2,1)S(1)}, bf16[1,4,128,4096]{3,2,1,0:T(8,128)(2,1)}, u32[]{:S(2)}) %copy-start.2) | copy-done | bytes 4194328
  54.5 4.4 %shard_map.107 = f32[32,128]{1,0:T(8,128)S(1)} custom-call(s32[8]{0:T(128)S(1)} %bitcast.109, s32[2,8]{1,0:T(2,128)S(1)} %bitcast.108, bf16[42,128,128]{2,1,0:T(8,128)(2,1)S(1)} %bitcast.107, bf16[4,128,4096]{2,1,0:T(8,128)(2,1)S(1)} %bitcast.105), custom_call_target="tpu_custom_call" | custom-call | flops 2147483648 | bytes 4194304 | tf_op jit(solution)/shard_map/pallas_call | solution.py:613
  58.9 0.1 slice.216
  59.0 0.1 reshape.144
  59.1 0.1 reshape.146.flip_ref
  59.2 0.1 min.8
  59.2 0.1 max.8
  59.4 0.1 slice.204
  59.5 0.1 fusion.19
  59.6 0.1 fusion.5.refs_0_
  59.6 5.7 %shard_map.108 = f32[7,4,8,128]{3,2,1,0:T(8,128)S(1)} custom-call(f32[4,8,128]{2,1,0:T(8,128)S(1)} %fusion.5.refs_0_), custom_call_target="tpu_custom_call" | custom-call | tf_op jit(solution)/shard_map/pallas_call | solution.py:211
  65.4 0.1 slice_bitcast_fusion.19
  65.5 0.1 slice_bitcast_fusion.18
  65.6 0.7 fusion.7
  66.3 0.1 fusion.9.v_ref
  66.4 2.2 %copy-done.3 = bf16[1,4,128,4096]{3,2,1,0:T(8,128)(2,1)S(1)} copy-done((bf16[1,4,128,4096]{3,2,1,0:T(8,128)(2,1)S(1)}, bf16[1,4,128,4096]{3,2,1,0:T(8,128)(2,1)}, u32[]{:S(2)}) %copy-start.3) | copy-done | bytes 4194328
  68.5 3.2 %shard_map.109.refs_0_ = bf16[6,128,128]{2,1,0:T(8,128)(2,1)S(1)} custom-call(bf16[4,128,4096]{2,1,0:T(8,128)(2,1)S(1)} %bitcast.106, f32[32,128]{1,0:T(8,128)S(1)} %fusion.9.v_ref), custom_call_target="tpu_custom_call" | custom-call | flops 2147483648 | bytes 4194304 | tf_op jit(solution)/shard_map/pallas_call | solution.py:626
  71.8 10.7 %shard_map.110 = bf16[7,6,128,128]{3,2,1,0:T(8,128)(2,1)S(1)} custom-call(bf16[6,128,128]{2,1,0:T(8,128)(2,1)S(1)} %shard_map.109.refs_0_), custom_call_target="tpu_custom_call" | custom-call | tf_op jit(solution)/shard_map/pallas_call | solution.py:211
  82.5 4.4 %shard_map.111.x_ref = bf16[64,128,128]{2,1,0:T(8,128)(2,1)S(1)} custom-call(s32[56]{0:T(128)S(1)} %get-tuple-element.49.bin_ref, s32[56]{0:T(128)S(1)} %get-tuple-element.50.col_ref, s32[56]{0:T(128)S(1)} %reshape.146.flip_ref, bf16[42,128,128]{2,1,0:T(8,128)(2,1)S(1)} %bitcast.101), custom_call_target="tpu_custom_call" | custom-call | flops 917504 | bytes 2097152 | tf_op jit(solution)/shard_map/pallas_call | solution.py:644
  86.9 36.2 %shard_map.112 = f32[8,128,128]{2,1,0:T(8,128)S(1)} custom-call(bf16[64,128,128]{2,1,0:T(8,128)(2,1)S(1)} %shard_map.111.x_ref), custom_call_target="tpu_custom_call" | custom-call | tf_op jit(solution)/shard_map/pallas_call | solution.py:552
  123.1 0.8 copy.21
  (25 shorter events, 0.2 us)
Async XLA Ops:
  4.0 1.0 copy-start
  30.6 0.7 copy-start.4
  31.3 5.3 %copy-start.1 = (f32[4,8,128]{2,1,0:T(8,128)S(1)}, f32[4,8,128]{2,1,0:T(8,128)}, u32[]{:S(2)}) copy-start(f32[4,8,128]{2,1,0:T(8,128)} %refs_1_.1) | copy-start | bytes 49156
  31.3 21.0 %copy-start.5 = (s32[1,2,8]{2,1,0:T(2,128)S(1)}, s32[1,2,8]{2,1,0:T(2,128)}, u32[]{:S(2)}) copy-start(s32[1,2,8]{2,1,0:T(2,128)} %param.15) | copy-start | bytes 196
  31.3 21.0 %copy-start.6 = (s32[1,8]{1,0:T(1,128)S(1)}, s32[1,8]{1,0:T(1,128)}, u32[]{:S(2)}) copy-start(s32[1,8]{1,0:T(1,128)} %param.13) | copy-start | bytes 100
  52.3 2.2 %copy-start.2 = (bf16[1,4,128,4096]{3,2,1,0:T(8,128)(2,1)S(1)}, bf16[1,4,128,4096]{3,2,1,0:T(8,128)(2,1)}, u32[]{:S(2)}) copy-start(bf16[1,4,128,4096]{3,2,1,0:T(8,128)(2,1)} %param.16) | copy-start | bytes 12582916
  66.4 2.2 %copy-start.3 = (bf16[1,4,128,4096]{3,2,1,0:T(8,128)(2,1)S(1)}, bf16[1,4,128,4096]{3,2,1,0:T(8,128)(2,1)}, u32[]{:S(2)}) copy-start(bf16[1,4,128,4096]{3,2,1,0:T(8,128)(2,1)} %param.16) | copy-start | bytes 12582916
